TPU v7x, 256 devices: a whole 4x4x8 slice. The times are simulated.
256 devices in a mesh: seq: 128 (over z, y, x_hi, core), chan: 2 (over x_lo).
Axes of the slice: x: 4 (x_hi: 2, x_lo: 2; x = x_hi * 2 + x_lo), y: 4, z: 8, core: 2. Of those that a mesh axis runs over, the one named last changes fastest.
Arguments:
- signal: bfloat16 [128, 65536], P('chan', 'seq'), may hold values from -6 to 6
- cotangent: bfloat16 [128, 65536], P('chan', 'seq'), may hold values from -18 to 18
- filters: bfloat16 [64, 65536], P(None, 'seq'), may hold values from -1.6 to 1.6
- skip: float32 [128], P('chan'), may hold values from -4 to 4
Outputs:
- signal_grad: bfloat16 [128, 65536], P('chan', 'seq')
- filter_grad: float32 [64, 65536], P('chan', 'seq')
- skip_grad: float32 [128], P('chan')
All inputs are finite; a program needn't handle non-finite values.
Results may differ from a plain program's by a relative error of at most 0.013.
Values may be sent and summed in bfloat16 or wider, within the bound.
A program may use at most 64 MiB of HBM per device.

v0:
```python
import math

import jax
import jax.numpy as jnp
from jax import lax
from jax.sharding import PartitionSpec as P


def shortened(shard):
    return jax.tree.map(lambda a: a.astype(jnp.bfloat16) if a.dtype == jnp.float32 else a, shard)


def counting(height):
    return jnp.arange(height, dtype=jnp.int32)


def row_order(devices):
    first_slot = counting(devices)
    second_slot = jnp.where(first_slot == 0, devices, 2 * devices - first_slot)
    return jnp.stack([first_slot, second_slot], axis=1).reshape(2 * devices)


def phase(left_idx, right_idx, period):
    product_idx = left_idx[:, None] * right_idx[None, :] % period
    angles = product_idx.astype(jnp.float32) * (2.0 * math.pi / period)
    return (jnp.cos(angles), jnp.sin(angles))


def rotate(real_part, imag_part, cosine, sine_tab, pattern, orient):
    real_cos = jnp.einsum(pattern, real_part, cosine, precision=lax.Precision.HIGHEST)
    real_sin = jnp.einsum(pattern, real_part, sine_tab, precision=lax.Precision.HIGHEST)
    imag_cos = jnp.einsum(pattern, imag_part, cosine, precision=lax.Precision.HIGHEST)
    imag_sin = jnp.einsum(pattern, imag_part, sine_tab, precision=lax.Precision.HIGHEST)
    return (real_cos - orient * imag_sin, imag_cos + orient * real_sin)


def twist(real_part, imag_part, cosine, sine_tab, orient):
    return (
        real_part * cosine - orient * imag_part * sine_tab,
        imag_part * cosine + orient * real_part * sine_tab,
    )


def split_length(length):
    return max((divisor for divisor in range(1, math.isqrt(length) + 1) if length % divisor == 0))


def local_forward(real_part, imag_part):
    channels, twins, length = real_part.shape
    slow_len = split_length(length)
    fast_len = length // slow_len
    real_part = real_part.reshape(channels, twins, slow_len, fast_len)
    imag_part = imag_part.reshape(channels, twins, slow_len, fast_len)
    cos_slow, sin_slow = phase(counting(slow_len), counting(slow_len), slow_len)
    real_part, imag_part = rotate(real_part, imag_part, cos_slow, sin_slow, "cjab,ak->cjkb", -1.0)
    cos_turn, sin_turn = phase(counting(slow_len), counting(fast_len), length)
    real_part, imag_part = twist(real_part, imag_part, cos_turn, sin_turn, -1.0)
    cos_fast, sin_fast = phase(counting(fast_len), counting(fast_len), fast_len)
    return rotate(real_part, imag_part, cos_fast, sin_fast, "cjkb,bl->cjkl", -1.0)


def local_inverse(real_part, imag_part):
    channels, twins, slow_len, fast_len = real_part.shape
    length = slow_len * fast_len
    cos_fast, sin_fast = phase(counting(fast_len), counting(fast_len), fast_len)
    real_part, imag_part = rotate(real_part, imag_part, cos_fast, sin_fast, "cjkl,lb->cjkb", 1.0)
    cos_turn, sin_turn = phase(counting(slow_len), counting(fast_len), length)
    real_part, imag_part = twist(real_part, imag_part, cos_turn, sin_turn, 1.0)
    cos_slow, sin_slow = phase(counting(slow_len), counting(slow_len), slow_len)
    real_part, imag_part = rotate(real_part, imag_part, cos_slow, sin_slow, "cjkb,ka->cjab", 1.0)
    return (real_part.reshape(channels, twins, length), imag_part.reshape(channels, twins, length))


def rows_forward(real_set, padded, offset, order):
    height = real_set.shape[1]
    cos_rows, sin_rows = phase(counting(height), order, 2 * height)
    real_vals = real_set.astype(jnp.float32)
    real_part = jnp.einsum("cpr,pk->ckr", real_vals, cos_rows, precision=lax.Precision.HIGHEST)
    imag_part = -jnp.einsum("cpr,pk->ckr", real_vals, sin_rows, precision=lax.Precision.HIGHEST)
    cos_turn, sin_turn = phase(order, offset + counting(real_set.shape[2]), padded)
    return twist(real_part, imag_part, cos_turn, sin_turn, -1.0)


def rows_inverse(real_part, imag_part, padded, offset, order):
    height = real_part.shape[1] // 2
    cos_turn, sin_turn = phase(order, offset + counting(real_part.shape[2]), padded)
    real_part, imag_part = twist(real_part, imag_part, cos_turn, sin_turn, 1.0)
    cos_rows, sin_rows = phase(order, counting(height), 2 * height)
    real_cos = jnp.einsum("ckr,kp->cpr", real_part, cos_rows, precision=lax.Precision.HIGHEST)
    imag_sin = jnp.einsum("ckr,kp->cpr", imag_part, sin_rows, precision=lax.Precision.HIGHEST)
    out_real = (real_cos - imag_sin) / padded
    return out_real


def local(signal, cotangent, filters, skip):
    channels, length = signal.shape
    devices = lax.axis_size("seq")
    offset = lax.axis_index("seq") * (length // devices)
    padded = 2 * length * devices
    order = row_order(devices)
    norm_factor = 1.0 / math.sqrt(length * devices)
    columns = (
        lax.all_to_all(
            signal.reshape(channels, 1, length), "seq", split_axis=2, concat_axis=1, tiled=True
        ),
        lax.all_to_all(
            cotangent.reshape(channels, 1, length), "seq", split_axis=2, concat_axis=1, tiled=True
        ),
        lax.all_to_all(
            filters.reshape(filters.shape[0], 1, length),
            "seq",
            split_axis=2,
            concat_axis=1,
            tiled=True,
        ),
    )
    row_spectra = [rows_forward(column_set, padded, offset, order) for column_set in columns]
    spread = (
        lax.all_to_all(
            row_spectra[0][0].astype(jnp.bfloat16), "seq", split_axis=1, concat_axis=2, tiled=True
        ).astype(jnp.float32),
        lax.all_to_all(
            row_spectra[0][1].astype(jnp.bfloat16), "seq", split_axis=1, concat_axis=2, tiled=True
        ).astype(jnp.float32),
        lax.all_to_all(
            row_spectra[1][0].astype(jnp.bfloat16), "seq", split_axis=1, concat_axis=2, tiled=True
        ).astype(jnp.float32),
        lax.all_to_all(
            row_spectra[1][1].astype(jnp.bfloat16), "seq", split_axis=1, concat_axis=2, tiled=True
        ).astype(jnp.float32),
        lax.all_to_all(
            row_spectra[2][0].astype(jnp.bfloat16), "seq", split_axis=1, concat_axis=2, tiled=True
        ).astype(jnp.float32),
        lax.all_to_all(
            row_spectra[2][1].astype(jnp.bfloat16), "seq", split_axis=1, concat_axis=2, tiled=True
        ).astype(jnp.float32),
    )
    signal_real, signal_imag = local_forward(spread[0], spread[1])
    cotan_real, cotan_imag = local_forward(spread[2], spread[3])
    filter_real, filter_imag = local_forward(spread[4], spread[5])
    conv_real = filter_real * cotan_real + filter_imag * cotan_imag
    conv_imag = filter_real * cotan_imag - filter_imag * cotan_real
    corr_real = signal_real * cotan_real + signal_imag * cotan_imag
    corr_imag = signal_real * cotan_imag - signal_imag * cotan_real
    cotan_val = cotangent.astype(jnp.float32)
    local_skip = jnp.sum(cotan_val * signal.astype(jnp.float32), axis=1)
    skip_grad = lax.psum(local_skip, "seq") * norm_factor
    back_conv_real, back_conv_imag = local_inverse(conv_real, conv_imag)
    back_corr_real, back_corr_imag = local_inverse(corr_real, corr_imag)
    arrived = (
        lax.all_to_all(
            shortened(back_conv_real), "seq", split_axis=2, concat_axis=1, tiled=True
        ).astype(back_conv_real.dtype),
        lax.all_to_all(
            shortened(back_conv_imag), "seq", split_axis=2, concat_axis=1, tiled=True
        ).astype(back_conv_imag.dtype),
        lax.all_to_all(
            shortened(back_corr_real), "seq", split_axis=2, concat_axis=1, tiled=True
        ).astype(back_corr_real.dtype),
        lax.all_to_all(
            shortened(back_corr_imag), "seq", split_axis=2, concat_axis=1, tiled=True
        ).astype(back_corr_imag.dtype),
    )
    time_conv = rows_inverse(arrived[0], arrived[1], padded, offset, order)
    time_corr = rows_inverse(arrived[2], arrived[3], padded, offset, order)
    placed = (
        lax.all_to_all(shortened(time_conv), "seq", split_axis=1, concat_axis=2, tiled=True).astype(
            time_conv.dtype
        ),
        lax.all_to_all(shortened(time_corr), "seq", split_axis=1, concat_axis=2, tiled=True).astype(
            time_corr.dtype
        ),
    )
    conv_time = placed[0].reshape(channels, length)
    filter_grad = (
        lax.psum_scatter(
            placed[1].reshape(channels, length).astype(jnp.bfloat16),
            "chan",
            scatter_dimension=0,
            tiled=True,
        ).astype(jnp.float32)
        * norm_factor
    )
    signal_grad = (conv_time + skip[:, None] * cotan_val).astype(jnp.bfloat16)
    return (signal_grad, filter_grad, skip_grad)


def solution(mesh):
    in_specs = (P("chan", "seq"), P("chan", "seq"), P(None, "seq"), P("chan"))
    out_specs = (P("chan", "seq"), P("chan", "seq"), P("chan"))
    return jax.shard_map(local, mesh=mesh, in_specs=in_specs, out_specs=out_specs, check_vma=False)
```

profile of v0, /device:TPU:1, one launch (start us, length us, event | category | flops | bytes accessed | tf_op | source)
XLA Modules:
  0.0 670.9 jit_solution(16680134016253449366)
XLA Ops:
  7.2 1.0 copy.333
  8.7 1.5 reduce
  10.9 16.4 %all-to-all-start.9 = ((bf16[128,2,128]{2,1,0:T(2,128)(2,1)}), bf16[128,2,128]{2,1,0:T(2,128)(2,1)S(1)}, u32[]{:S(2)}, u32[]{:S(2)}) async-start(bf16[128,2,128]{2,1,0:T(2,128)(2,1)} %reshape.263), calls=%async_computation.9 | async-start | bytes 131072 | tf_op jit(solution)/shard_map/all_to_all | solution.py:103
  28.4 1.5 reduce.1
  30.9 1.5 reduce.2
  33.3 5.7 all-to-all-done.9
  39.0 8.0 %all-to-all-start.3 = ((bf16[128,2,128]{2,1,0:T(2,128)(2,1)}), bf16[128,2,128]{2,1,0:T(2,128)(2,1)S(1)}, u32[]{:S(2)}, u32[]{:S(2)}) async-start(bf16[128,2,128]{2,1,0:T(2,128)(2,1)} %reshape.253), calls=%async_computation.3 | async-start | bytes 131072 | tf_op jit(solution)/shard_map/all_to_all | solution.py:106
  48.9 9.9 %all-to-all-done.3 = bf16[128,2,128]{2,1,0:T(2,128)(2,1)S(1)} async-done(((bf16[128,2,128]{2,1,0:T(2,128)(2,1)}), bf16[128,2,128]{2,1,0:T(2,128)(2,1)S(1)}, u32[]{:S(2)}, u32[]{:S(2)}) %all-to-all-start.3) | async-done | bytes 65568 | tf_op jit(solution)/shard_map/all_to_all | solution.py:106
  58.7 6.5 all-to-all-start
  67.1 10.0 %all-to-all-done = bf16[128,2,128]{2,1,0:T(2,128)(2,1)S(1)} async-done(((bf16[128,2,128]{2,1,0:T(2,128)(2,1)}), bf16[128,2,128]{2,1,0:T(2,128)(2,1)S(1)}, u32[]{:S(2)}, u32[]{:S(2)}) %all-to-all-start) | async-done | bytes 65568 | tf_op jit(solution)/shard_map/all_to_all | solution.py:109
  79.2 0.9 reshape.255
  80.1 6.2 all-to-all-start.4
  87.4 12.1 %all-to-all-done.4 = bf16[128,2,256]{2,1,0:T(2,128)(2,1)S(1)} async-done(((bf16[128,2,256]{2,1,0:T(2,128)(2,1)}), bf16[128,2,256]{2,1,0:T(2,128)(2,1)S(1)}, u32[]{:S(2)}, u32[]{:S(2)}) %all-to-all-start.4) | async-done | bytes 131104 | tf_op jit(solution)/shard_map/all_to_all | solution.py:125
  99.4 6.3 all-to-all-start.5
  106.5 0.9 reshape.251
  107.4 11.4 %all-to-all-done.5 = bf16[128,2,256]{2,1,0:T(2,128)(2,1)S(1)} async-done(((bf16[128,2,256]{2,1,0:T(2,128)(2,1)}), bf16[128,2,256]{2,1,0:T(2,128)(2,1)S(1)}, u32[]{:S(2)}, u32[]{:S(2)}) %all-to-all-start.5) | async-done | bytes 131104 | tf_op jit(solution)/shard_map/all_to_all | solution.py:128
  118.8 6.6 all-to-all-start.1
  131.4 7.1 %all-to-all-done.1 = bf16[128,2,256]{2,1,0:T(2,128)(2,1)S(1)} async-done(((bf16[128,2,256]{2,1,0:T(2,128)(2,1)}), bf16[128,2,256]{2,1,0:T(2,128)(2,1)S(1)}, u32[]{:S(2)}, u32[]{:S(2)}) %all-to-all-start.1) | async-done | bytes 131104 | tf_op jit(solution)/shard_map/all_to_all | solution.py:131
  138.5 6.8 %all-to-all-start.2 = ((bf16[128,2,256]{2,1,0:T(2,128)(2,1)}), bf16[128,2,256]{2,1,0:T(2,128)(2,1)S(1)}, u32[]{:S(2)}, u32[]{:S(2)}) async-start(bf16[128,2,256]{2,1,0:T(2,128)(2,1)} %reshape.249), calls=%async_computation.2 | async-start | bytes 262144 | tf_op jit(solution)/shard_map/all_to_all | solution.py:134
  147.0 11.2 %all-to-all-done.2 = bf16[128,2,256]{2,1,0:T(2,128)(2,1)S(1)} async-done(((bf16[128,2,256]{2,1,0:T(2,128)(2,1)}), bf16[128,2,256]{2,1,0:T(2,128)(2,1)S(1)}, u32[]{:S(2)}, u32[]{:S(2)}) %all-to-all-start.2) | async-done | bytes 131104 | tf_op jit(solution)/shard_map/all_to_all | solution.py:134
  158.2 6.3 all-to-all-start.11
  165.8 11.8 %all-to-all-done.11 = bf16[128,2,256]{2,1,0:T(2,128)(2,1)S(1)} async-done(((bf16[128,2,256]{2,1,0:T(2,128)(2,1)}), bf16[128,2,256]{2,1,0:T(2,128)(2,1)S(1)}, u32[]{:S(2)}, u32[]{:S(2)}) %all-to-all-start.11) | async-done | bytes 131104 | tf_op jit(solution)/shard_map/all_to_all | solution.py:122
  177.6 7.7 %all-to-all-start.10 = ((bf16[128,2,256]{2,1,0:T(2,128)(2,1)}), bf16[128,2,256]{2,1,0:T(2,128)(2,1)}, u32[]{:S(2)}, u32[]{:S(2)}) async-start(bf16[128,2,256]{2,1,0:T(2,128)(2,1)} %reshape.267), calls=%async_computation.10 | async-start | bytes 262144 | tf_op jit(solution)/shard_map/all_to_all | solution.py:119
  185.8 1.2 convolution_multiply_fusion.1
  187.4 10.2 %all-to-all-done.10 = bf16[128,2,256]{2,1,0:T(2,128)(2,1)} async-done(((bf16[128,2,256]{2,1,0:T(2,128)(2,1)}), bf16[128,2,256]{2,1,0:T(2,128)(2,1)}, u32[]{:S(2)}, u32[]{:S(2)}) %all-to-all-start.10) | async-done | bytes 131104 | tf_op jit(solution)/shard_map/all_to_all | solution.py:119
  197.6 1.1 reshape.268
  210.5 1.2 multiply_subtract_fusion.1
  216.4 0.9 multiply_subtract_fusion
  220.3 6.6 all-to-all-start.12
  229.0 0.9 reshape.271
  229.8 10.1 %all-to-all-done.12 = bf16[128,2,256]{2,1,0:T(2,128)(2,1)S(1)} async-done(((bf16[128,2,256]{2,1,0:T(2,128)(2,1)}), bf16[128,2,256]{2,1,0:T(2,128)(2,1)S(1)}, u32[]{:S(2)}, u32[]{:S(2)}) %all-to-all-start.12) | async-done | bytes 131104 | tf_op jit(solution)/shard_map/all_to_all | solution.py:157
  239.9 6.2 all-to-all-start.13
  249.1 10.2 %all-to-all-done.13 = bf16[128,2,256]{2,1,0:T(2,128)(2,1)S(1)} async-done(((bf16[128,2,256]{2,1,0:T(2,128)(2,1)}), bf16[128,2,256]{2,1,0:T(2,128)(2,1)S(1)}, u32[]{:S(2)}, u32[]{:S(2)}) %all-to-all-start.13) | async-done | bytes 131104 | tf_op jit(solution)/shard_map/all_to_all | solution.py:160
  259.3 6.6 all-to-all-start.6
  268.0 0.9 reshape.261
  270.8 8.2 %all-to-all-done.6 = bf16[128,2,256]{2,1,0:T(2,128)(2,1)S(1)} async-done(((bf16[128,2,256]{2,1,0:T(2,128)(2,1)}), bf16[128,2,256]{2,1,0:T(2,128)(2,1)S(1)}, u32[]{:S(2)}, u32[]{:S(2)}) %all-to-all-start.6) | async-done | bytes 131104 | tf_op jit(solution)/shard_map/all_to_all | solution.py:151
  279.0 6.2 all-to-all-start.7
  285.9 1.5 fusion.23
  287.4 1.5 fusion.18
  290.8 7.5 %all-to-all-done.7 = bf16[128,2,256]{2,1,0:T(2,128)(2,1)S(1)} async-done(((bf16[128,2,256]{2,1,0:T(2,128)(2,1)}), bf16[128,2,256]{2,1,0:T(2,128)(2,1)S(1)}, u32[]{:S(2)}, u32[]{:S(2)}) %all-to-all-start.7) | async-done | bytes 131104 | tf_op jit(solution)/shard_map/all_to_all | solution.py:154
  298.3 6.8 %all-to-all-start.14 = ((bf16[128,2,128]{2,1,0:T(2,128)(2,1)}), bf16[128,2,128]{2,1,0:T(2,128)(2,1)S(1)}, u32[]{:S(2)}, u32[]{:S(2)}) async-start(bf16[128,2,128]{2,1,0:T(2,128)(2,1)} %reshape.275), calls=%async_computation.14 | async-start | bytes 131072 | tf_op jit(solution)/shard_map/all_to_all | solution.py:170
  306.0 1.5 fusion.30
  307.6 1.6 fusion.19
  310.1 6.8 %all-to-all-done.14 = bf16[128,2,128]{2,1,0:T(2,128)(2,1)S(1)} async-done(((bf16[128,2,128]{2,1,0:T(2,128)(2,1)}), bf16[128,2,128]{2,1,0:T(2,128)(2,1)S(1)}, u32[]{:S(2)}, u32[]{:S(2)}) %all-to-all-start.14) | async-done | bytes 65568 | tf_op jit(solution)/shard_map/all_to_all | solution.py:170
  316.8 7.2 %all-to-all-start.8 = ((bf16[128,2,128]{2,1,0:T(2,128)(2,1)}), bf16[128,2,128]{2,1,0:T(2,128)(2,1)S(1)}, u32[]{:S(2)}, u32[]{:S(2)}) async-start(bf16[128,2,128]{2,1,0:T(2,128)(2,1)} %reshape.273), calls=%async_computation.8 | async-start | bytes 131072 | tf_op jit(solution)/shard_map/all_to_all | solution.py:167
  325.8 9.8 %all-to-all-done.8 = bf16[128,2,128]{2,1,0:T(2,128)(2,1)S(1)} async-done(((bf16[128,2,128]{2,1,0:T(2,128)(2,1)}), bf16[128,2,128]{2,1,0:T(2,128)(2,1)S(1)}, u32[]{:S(2)}, u32[]{:S(2)}) %all-to-all-start.8) | async-done | bytes 65568 | tf_op jit(solution)/shard_map/all_to_all | solution.py:167
  337.3 324.1 %psum.7 = f32[64]{0:T(128)S(1)} all-reduce(f32[64]{0:T(128)S(1)} %get-tuple-element.37), channel_id=1, replica_groups=mesh['seq'=128,'chan'=2] {'seq'}, use_global_device_ids=true, to_apply=%region_2.3 | all-reduce | flops 64 | bytes 512 | tf_op jit(solution)/shard_map/psum | solution.py:147
  661.9 0.9 copy.379
  (161 shorter events, 58.1 us)
Async XLA Ops:
  10.9 28.1 %all-to-all-start.9 = ((bf16[128,2,128]{2,1,0:T(2,128)(2,1)}), bf16[128,2,128]{2,1,0:T(2,128)(2,1)S(1)}, u32[]{:S(2)}, u32[]{:S(2)}) async-start(bf16[128,2,128]{2,1,0:T(2,128)(2,1)} %reshape.263), calls=%async_computation.9 | async-start | bytes 131072 | tf_op jit(solution)/shard_map/all_to_all | solution.py:103
  27.4 0.8 copy-start.1
  27.6 50.5 %copy-start.7 = (s32[256]{0:T(256)}, s32[256]{0:T(256)S(1)}, u32[]{:S(2)}) copy-start(s32[256]{0:T(256)S(1)} %mul.1168) | copy-start | bytes 3076
  29.9 0.8 copy-start.6
  39.0 19.7 %all-to-all-start.3 = ((bf16[128,2,128]{2,1,0:T(2,128)(2,1)}), bf16[128,2,128]{2,1,0:T(2,128)(2,1)S(1)}, u32[]{:S(2)}, u32[]{:S(2)}) async-start(bf16[128,2,128]{2,1,0:T(2,128)(2,1)} %reshape.253), calls=%async_computation.3 | async-start | bytes 131072 | tf_op jit(solution)/shard_map/all_to_all | solution.py:106
  58.7 18.4 %all-to-all-start = ((bf16[128,2,128]{2,1,0:T(2,128)(2,1)}), bf16[128,2,128]{2,1,0:T(2,128)(2,1)S(1)}, u32[]{:S(2)}, u32[]{:S(2)}) async-start(bf16[128,2,128]{2,1,0:T(2,128)(2,1)} %reshape.247), calls=%async_computation | async-start | bytes 131072 | tf_op jit(solution)/shard_map/all_to_all | solution.py:109
  80.1 19.3 %all-to-all-start.4 = ((bf16[128,2,256]{2,1,0:T(2,128)(2,1)}), bf16[128,2,256]{2,1,0:T(2,128)(2,1)S(1)}, u32[]{:S(2)}, u32[]{:S(2)}) async-start(bf16[128,2,256]{2,1,0:T(2,128)(2,1)} %reshape.255), calls=%async_computation.4 | async-start | bytes 262144 | tf_op jit(solution)/shard_map/all_to_all | solution.py:125
  99.4 19.4 %all-to-all-start.5 = ((bf16[128,2,256]{2,1,0:T(2,128)(2,1)}), bf16[128,2,256]{2,1,0:T(2,128)(2,1)S(1)}, u32[]{:S(2)}, u32[]{:S(2)}) async-start(bf16[128,2,256]{2,1,0:T(2,128)(2,1)} %reshape.257), calls=%async_computation.5 | async-start | bytes 262144 | tf_op jit(solution)/shard_map/all_to_all | solution.py:128
  118.8 19.7 %all-to-all-start.1 = ((bf16[128,2,256]{2,1,0:T(2,128)(2,1)}), bf16[128,2,256]{2,1,0:T(2,128)(2,1)S(1)}, u32[]{:S(2)}, u32[]{:S(2)}) async-start(bf16[128,2,256]{2,1,0:T(2,128)(2,1)} %reshape.251), calls=%async_computation.1 | async-start | bytes 262144 | tf_op jit(solution)/shard_map/all_to_all | solution.py:131
  138.5 19.7 %all-to-all-start.2 = ((bf16[128,2,256]{2,1,0:T(2,128)(2,1)}), bf16[128,2,256]{2,1,0:T(2,128)(2,1)S(1)}, u32[]{:S(2)}, u32[]{:S(2)}) async-start(bf16[128,2,256]{2,1,0:T(2,128)(2,1)} %reshape.249), calls=%async_computation.2 | async-start | bytes 262144 | tf_op jit(solution)/shard_map/all_to_all | solution.py:134
  158.2 19.4 %all-to-all-start.11 = ((bf16[128,2,256]{2,1,0:T(2,128)(2,1)}), bf16[128,2,256]{2,1,0:T(2,128)(2,1)S(1)}, u32[]{:S(2)}, u32[]{:S(2)}) async-start(bf16[128,2,256]{2,1,0:T(2,128)(2,1)} %reshape.265), calls=%async_computation.11 | async-start | bytes 262144 | tf_op jit(solution)/shard_map/all_to_all | solution.py:122
  177.6 20.0 %all-to-all-start.10 = ((bf16[128,2,256]{2,1,0:T(2,128)(2,1)}), bf16[128,2,256]{2,1,0:T(2,128)(2,1)}, u32[]{:S(2)}, u32[]{:S(2)}) async-start(bf16[128,2,256]{2,1,0:T(2,128)(2,1)} %reshape.267), calls=%async_computation.10 | async-start | bytes 262144 | tf_op jit(solution)/shard_map/all_to_all | solution.py:119
  199.0 1.0 copy-start
  200.5 0.7 copy-start.4
  200.5 0.7 copy-start.5
  215.7 0.7 copy-start.9
  220.3 19.7 %all-to-all-start.12 = ((bf16[128,2,256]{2,1,0:T(2,128)(2,1)}), bf16[128,2,256]{2,1,0:T(2,128)(2,1)S(1)}, u32[]{:S(2)}, u32[]{:S(2)}) async-start(bf16[128,2,256]{2,1,0:T(2,128)(2,1)} %reshape.269), calls=%async_computation.12 | async-start | bytes 262144 | tf_op jit(solution)/shard_map/all_to_all | solution.py:157
  239.9 19.4 %all-to-all-start.13 = ((bf16[128,2,256]{2,1,0:T(2,128)(2,1)}), bf16[128,2,256]{2,1,0:T(2,128)(2,1)S(1)}, u32[]{:S(2)}, u32[]{:S(2)}) async-start(bf16[128,2,256]{2,1,0:T(2,128)(2,1)} %reshape.271), calls=%async_computation.13 | async-start | bytes 262144 | tf_op jit(solution)/shard_map/all_to_all | solution.py:160
  259.3 19.7 %all-to-all-start.6 = ((bf16[128,2,256]{2,1,0:T(2,128)(2,1)}), bf16[128,2,256]{2,1,0:T(2,128)(2,1)S(1)}, u32[]{:S(2)}, u32[]{:S(2)}) async-start(bf16[128,2,256]{2,1,0:T(2,128)(2,1)} %reshape.259), calls=%async_computation.6 | async-start | bytes 262144 | tf_op jit(solution)/shard_map/all_to_all | solution.py:151
  279.0 19.4 %all-to-all-start.7 = ((bf16[128,2,256]{2,1,0:T(2,128)(2,1)}), bf16[128,2,256]{2,1,0:T(2,128)(2,1)S(1)}, u32[]{:S(2)}, u32[]{:S(2)}) async-start(bf16[128,2,256]{2,1,0:T(2,128)(2,1)} %reshape.261), calls=%async_computation.7 | async-start | bytes 262144 | tf_op jit(solution)/shard_map/all_to_all | solution.py:154
  285.2 0.7 copy-start.8
  298.3 18.5 %all-to-all-start.14 = ((bf16[128,2,128]{2,1,0:T(2,128)(2,1)}), bf16[128,2,128]{2,1,0:T(2,128)(2,1)S(1)}, u32[]{:S(2)}, u32[]{:S(2)}) async-start(bf16[128,2,128]{2,1,0:T(2,128)(2,1)} %reshape.275), calls=%async_computation.14 | async-start | bytes 131072 | tf_op jit(solution)/shard_map/all_to_all | solution.py:170
  310.1 14.0 %copy-start.2 = (bf16[64,512]{1,0:T(8,128)(2,1)S(1)}, bf16[64,512]{1,0:T(8,128)(2,1)}, u32[]{:S(2)}) copy-start(bf16[64,512]{1,0:T(8,128)(2,1)} %param.5) | copy-start | bytes 196612
  316.8 18.9 %all-to-all-start.8 = ((bf16[128,2,128]{2,1,0:T(2,128)(2,1)}), bf16[128,2,128]{2,1,0:T(2,128)(2,1)S(1)}, u32[]{:S(2)}, u32[]{:S(2)}) async-start(bf16[128,2,128]{2,1,0:T(2,128)(2,1)} %reshape.273), calls=%async_computation.8 | async-start | bytes 131072 | tf_op jit(solution)/shard_map/all_to_all | solution.py:167
  324.0 0.8 copy-start.3
  324.0 337.9 %reduce-scatter.4.cloned.1.call-start = ((), (), s32[]{:S(2)}) async-start(), calls=%async_computation.16 | async-start | bytes 98304
  335.8 0.7 copy-start.10
Sparse Core Ops, SparseCore 0:
  327.3 15.6 reduce-scatter.3
where the time goes:
time: 680 us; the launch traced here: 671 us
  blocking collectives  324 us (48%)
  waiting for transfers between devices  142 us (21%)
  starting transfers between devices  111 us (16%)
  matrix products  39 us (6%)
  local copies, waits for them, and re-layouts  33.6 us (5%)
  between operations  15.7 us (2%)
    psum x1, blocking collectives, local(): skip_grad = lax.psum(local_skip, 'seq') * norm_factor  324 us
    unnamed x62, local copies, waits for them, and re-layouts  23.4 us
    all_to_all x1, starting transfers between devices, local(): lax.all_to_all(signal.reshape(channels, 1, length), 'seq', split_axis=2,...  16.4 us
  transfers between devices with their start and end apart: 16, of which 15 were waited for; matrix products, arithmetic and copies ran while one was open for 7% of the time, Pallas kernels for 0%

commit v1 on v0

v1 whole, which is shorter than its diff:
```python
import functools
import math

import jax
import jax.numpy as jnp
import ml_dtypes
import numpy as np
from jax import lax
from jax.experimental import pallas as pl
from jax.experimental.pallas import tpu as pltpu
from jax.sharding import PartitionSpec as P

MESH = pl.DeviceIdType.MESH
F32, BF16 = jnp.float32, jnp.bfloat16
CHIPS, CORES, LANES, ROWS, QUADS = 64, 2, 128, 512, 4
KBLOCK = 256


def high_low(table):
    high = table.astype(ml_dtypes.bfloat16)
    low = (table - high.astype(np.float64)).astype(ml_dtypes.bfloat16)
    return np.stack([high, low])


@functools.lru_cache(None)
def tables():
    k1 = np.arange(ROWS)
    row_angle = np.pi * ((2 * k1[:, None] + 1) * np.arange(ROWS)[None, :] % 2048) / 1024.0
    blocks = ROWS // KBLOCK
    cos_rows = np.cos(row_angle).reshape(blocks, KBLOCK, ROWS)
    sin_rows = np.sin(row_angle).reshape(blocks, KBLOCK, ROWS)
    rows_fwd = high_low(np.concatenate([cos_rows, -sin_rows], axis=1))
    back = np.concatenate([np.cos(row_angle).T, -np.sin(row_angle).T], axis=1)
    back = back.reshape(CHIPS, CORES, QUADS, 2 * ROWS).transpose(1, 0, 2, 3)
    rows_inv = high_low(back.reshape(CORES, CHIPS * QUADS, 2 * ROWS))
    lane = np.arange(LANES)
    lane_angle = 2.0 * np.pi * (lane[:, None] * lane[None, :] % LANES) / LANES
    cos, sin = np.cos(lane_angle), np.sin(lane_angle)
    lanes_fwd = high_low(np.block([[cos, -sin], [sin, cos]]))
    lanes_inv = high_low(np.block([[cos, sin], [-sin, cos]]))
    turn = np.pi * (2 * k1[:, None] + 1) * lane[None, :] / 131072.0
    turns = np.stack([np.cos(turn), np.sin(turn)]).astype(np.float32)
    return rows_fwd, rows_inv, np.stack([lanes_fwd, lanes_inv]), turns


def split(x):
    high = x.astype(BF16)
    return high, (x - high.astype(F32)).astype(BF16)


def dot(a, b):
    return jnp.dot(a, b, preferred_element_type=F32)


def three_pass(x, high, low):
    x_high, x_low = split(x)
    return dot(x_high, high) + dot(x_low, high) + dot(x_high, low)


def kernel(
    signal_hbm, cotan_hbm, filter_hbm, skip_ref, rows_fwd_hbm, rows_inv_hbm, lanes_hbm, turns_hbm,
    signal_out, filter_out, skip_out,
    signal_in, cotan_in, filter_in, rows_fwd, rows_inv, lanes_tab, turns,
    stage, sent, got, mate, packed, spectrum, keep, give, mate_y, side_y, message, final,
    part, part_mate, part_plane, part_plane_sum, part_line,
    load_sem, table_sem, send_sem, recv_sem, mate_sems, back_sems, out_send, out_recv, part_send, part_recv,
):
    me, chan = lax.axis_index("seq"), lax.axis_index("chan")
    core, chip = me % 2, me // 2
    other_core, other_chan = 1 - core, 1 - chan
    z, y, x = chip // 8, (chip // 2) % 4, chip % 2
    is_home = chip // 32 == chan
    not_home = chip // 32 != chan

    def device(chip_id):
        return (2 * chip_id + core, chan)

    mate_id = (2 * chip + other_core, chan)

    loads = [
        pltpu.make_async_copy(src, dst, load_sem.at[i])
        for i, (src, dst) in enumerate(
            ((signal_hbm, signal_in), (cotan_hbm, cotan_in), (filter_hbm, filter_in))
        )
    ]
    for load in loads:
        load.start()
    table_loads = [
        pltpu.make_async_copy(src, dst, table_sem.at[i])
        for i, (src, dst) in enumerate(
            (
                (rows_fwd_hbm, rows_fwd),
                (rows_inv_hbm, rows_inv),
                (lanes_hbm, lanes_tab),
                (turns_hbm, turns),
            )
        )
    ]
    for load in table_loads:
        load.start()

    def far_first(i):
        kz, ky, kx = i // 8, (i // 2) % 4, i % 2
        dz = 4 + (1 - 2 * (kz % 2)) * ((kz + 1) // 2)
        dy = 2 + (1 - 2 * (ky % 2)) * ((ky + 1) // 2)
        dx = 1 - kx
        return ((z + dz) % 8 * 4 + (y + dy) % 4) * 2 + (x + dx) % 2

    barrier = pltpu.get_barrier_semaphore()

    def greet(i, carry):
        pl.semaphore_signal(barrier, inc=1, device_id=device(far_first(i)), device_id_type=MESH)
        return carry

    lax.fori_loop(0, CHIPS - 1, greet, 0, unroll=7)
    pl.semaphore_signal(barrier, inc=1, device_id=mate_id, device_id_type=MESH)
    for c in range(CORES):
        pl.semaphore_signal(
            barrier, inc=1, device_id=(2 * chip + c, other_chan), device_id_type=MESH
        )

    for load in loads:
        load.wait()
    signal_val = signal_in[...].astype(F32)
    cotan_val = cotan_in[...].astype(F32)
    filter_val = filter_in[...].astype(F32)
    for q in range(QUADS):
        lanes = slice(q * LANES, (q + 1) * LANES)
        stage[0, pl.ds(q, CHIPS, stride=8), :] = signal_val[:, lanes]
        stage[0, pl.ds(4 + q, CHIPS, stride=8), :] = cotan_val[:, lanes]
        stage[1, pl.ds(q, CHIPS, stride=8), :] = filter_val[:, lanes]
        stage[1, pl.ds(4 + q, CHIPS, stride=8), :] = cotan_val[:, lanes]
    for half in range(2):
        sent[:, half] = stage[half].reshape(CHIPS, 8, LANES).astype(BF16)
    sums = jnp.sum(signal_val * cotan_val, axis=1, keepdims=True)
    diagonal = lax.broadcasted_iota(jnp.int32, (CHIPS, LANES), 0) == lax.broadcasted_iota(
        jnp.int32, (CHIPS, LANES), 1
    )
    row = jnp.sum(jnp.where(diagonal, sums, 0.0), axis=0, keepdims=True)
    part[...] = jnp.broadcast_to(row, (8, LANES))

    pl.semaphore_wait(barrier, CHIPS + 2)

    def send(i, carry):
        to = far_first(i)
        pltpu.make_async_remote_copy(
            src_ref=sent.at[to], dst_ref=got.at[chip], send_sem=send_sem, recv_sem=recv_sem,
            device_id=device(to), device_id_type=MESH,
        ).start()
        return carry

    lax.fori_loop(0, CHIPS - 1, send, 0, unroll=7)
    got[chip] = sent[chip]

    mate_part = pltpu.make_async_remote_copy(
        src_ref=part, dst_ref=part_mate, send_sem=part_send.at[0], recv_sem=part_recv.at[0],
        device_id=mate_id, device_id_type=MESH,
    )
    mate_part.start()
    mate_part.wait()
    part[...] = part[...] + part_mate[...]
    spot = chip % 8

    def send_plane(i, carry):
        to = (spot + i) % 8
        pltpu.make_async_remote_copy(
            src_ref=part, dst_ref=part_plane.at[spot], send_sem=part_send.at[1], recv_sem=part_recv.at[1],
            device_id=device(chip // 8 * 8 + to), device_id_type=MESH,
        ).start()
        return carry

    lax.fori_loop(1, 8, send_plane, 0)

    all_but_one = got.at[pl.ds(0, CHIPS - 1)]
    pltpu.make_async_copy(all_but_one, all_but_one, send_sem).wait()
    pltpu.make_async_copy(all_but_one, all_but_one, recv_sem).wait()

    swap = pltpu.make_async_remote_copy(
        src_ref=got.at[:, core], dst_ref=mate, send_sem=mate_sems.at[0], recv_sem=mate_sems.at[1],
        device_id=mate_id, device_id_type=MESH,
    )
    swap.start()

    seven = part_plane.at[pl.ds(0, 7)]
    pltpu.make_async_copy(seven, seven, part_send.at[1]).wait()
    pltpu.make_async_copy(seven, seven, part_recv.at[1]).wait()
    part_plane[spot] = part[...]
    part_plane_sum[...] = jnp.sum(part_plane[...], axis=0)

    def send_line(i, carry):
        to = (z + i) % 8
        pltpu.make_async_remote_copy(
            src_ref=part_plane_sum, dst_ref=part_line.at[z], send_sem=part_send.at[2], recv_sem=part_recv.at[2],
            device_id=device(to * 8 + spot), device_id_type=MESH,
        ).start()
        return carry

    lax.fori_loop(1, 8, send_line, 0)
    for load in table_loads:
        load.wait()
    swap.wait()

    ours = got[:, other_core].astype(F32)
    theirs = mate[...].astype(F32)
    first = jnp.where(core == 0, ours, theirs)
    second = jnp.where(core == 0, theirs, ours)
    for k in range(2):
        rows = slice(4 * k, 4 * k + 4)
        both = jnp.concatenate([first[:, rows], second[:, rows]], axis=1)
        packed[:, k * LANES : (k + 1) * LANES] = both.reshape(ROWS, LANES).astype(BF16)

    def block(b, carry):
        span = pl.ds(b * KBLOCK, KBLOCK)
        cos, sin = turns[0, span, :], turns[1, span, :]
        right = packed[...]
        waves = dot(rows_fwd[0, b], right) + dot(rows_fwd[1, b], right)
        real, imag = waves[:KBLOCK], waves[KBLOCK:]
        cos2 = jnp.concatenate([cos, cos], axis=1)
        sin2 = jnp.concatenate([sin, sin], axis=1)
        real, imag = real * cos2 + imag * sin2, imag * cos2 - real * sin2
        left = jnp.concatenate(
            [
                jnp.concatenate([real[:, :LANES], imag[:, :LANES]], axis=1),
                jnp.concatenate([real[:, LANES:], imag[:, LANES:]], axis=1),
            ],
            axis=0,
        )
        freq = three_pass(left, lanes_tab[0, 0], lanes_tab[0, 1])
        b_real, b_imag = freq[:KBLOCK, :LANES], freq[:KBLOCK, LANES:]
        g_real, g_imag = freq[KBLOCK:, :LANES], freq[KBLOCK:, LANES:]
        product = jnp.concatenate(
            [b_real * g_real + b_imag * g_imag, b_real * g_imag - b_imag * g_real], axis=1
        )
        inner = three_pass(product, lanes_tab[1, 0], lanes_tab[1, 1])
        real, imag = inner[:, :LANES], inner[:, LANES:]
        real, imag = real * cos - imag * sin, imag * cos + real * sin
        for k, value in enumerate((real, imag)):
            high, low = split(value)
            spectrum[pl.ds(k * ROWS + b * KBLOCK, KBLOCK), :LANES] = high
            spectrum[pl.ds(k * ROWS + b * KBLOCK, KBLOCK), LANES:] = low
        return carry

    lax.fori_loop(0, ROWS // KBLOCK, block, 0)

    def rows_of(parity):
        wide = dot(rows_inv[0, parity], spectrum[...])
        value = wide[:, :LANES] + wide[:, LANES:] + dot(rows_inv[1, parity], spectrum[:, :LANES])
        return (value * (2.0 / 131072.0)).reshape(CHIPS, QUADS, LANES).astype(BF16)

    give[...] = rows_of(other_core)
    to_mate = pltpu.make_async_remote_copy(
        src_ref=give, dst_ref=mate_y, send_sem=back_sems.at[0], recv_sem=back_sems.at[1],
        device_id=mate_id, device_id_type=MESH,
    )
    to_side_give = pltpu.make_async_remote_copy(
        src_ref=give, dst_ref=side_y, send_sem=back_sems.at[2], recv_sem=back_sems.at[4],
        device_id=(2 * chip + other_core, other_chan), device_id_type=MESH,
    )
    to_side_keep = pltpu.make_async_remote_copy(
        src_ref=keep, dst_ref=side_y, send_sem=back_sems.at[3], recv_sem=back_sems.at[4],
        device_id=(me, other_chan), device_id_type=MESH,
    )
    giver = jnp.logical_or(is_home, core == 0)
    sider = jnp.logical_and(not_home, core == 1)

    @pl.when(giver)
    def _():
        to_mate.start()

    @pl.when(sider)
    def _():
        to_side_give.start()

    keep[...] = rows_of(core)

    @pl.when(sider)
    def _():
        to_side_keep.start()
        to_side_give.wait_send()
        to_side_keep.wait_send()

    @pl.when(giver)
    def _():
        to_mate.wait_send()

    @pl.when(jnp.logical_or(is_home, core == 1))
    def _():
        to_mate.wait_recv()

    @pl.when(is_home)
    def _():
        to_side_keep.wait_recv()
        mine, others = keep[...].astype(F32), mate_y[...].astype(F32)
        message[:, 0] = jnp.where(core == 0, mine, others).astype(BF16)
        message[:, 1] = (jnp.where(core == 0, others, mine) + side_y[...].astype(F32)).astype(BF16)

        def send_back(i, carry):
            to = far_first(i)
            pltpu.make_async_remote_copy(
                src_ref=message.at[to], dst_ref=final.at[chip], send_sem=out_send.at[0], recv_sem=out_recv.at[0],
                device_id=device(to), device_id_type=MESH,
            ).start()
            return carry

        lax.fori_loop(0, CHIPS - 1, send_back, 0, unroll=7)

    @pl.when(jnp.logical_and(not_home, core == 0))
    def _():
        message[:, 0] = keep[...]

    @pl.when(jnp.logical_and(not_home, core == 1))
    def _():
        message[:, 0] = mate_y[...]

    @pl.when(not_home)
    def _():
        def send_back(i, carry):
            to = far_first(i)
            pltpu.make_async_remote_copy(
                src_ref=message.at[to, 0], dst_ref=final.at[chip, 0], send_sem=out_send.at[1], recv_sem=out_recv.at[1],
                device_id=device(to), device_id_type=MESH,
            ).start()
            return carry

        lax.fori_loop(0, CHIPS - 1, send_back, 0, unroll=7)

    line = part_line.at[pl.ds(0, 7)]
    pltpu.make_async_copy(line, line, part_send.at[2]).wait()
    pltpu.make_async_copy(line, line, part_recv.at[2]).wait()
    part_line[z] = part_plane_sum[...]
    skip_out[...] = jnp.sum(part_line[...], axis=0)[:1] * (1.0 / 256.0)

    skip_col = jnp.sum(
        jnp.where(diagonal, jnp.broadcast_to(skip_ref[...], (CHIPS, LANES)), 0.0), axis=1, keepdims=True
    )
    for q in range(QUADS):
        lanes = slice(q * LANES, (q + 1) * LANES)
        stage[0, pl.ds(q, CHIPS, stride=8), :] = cotan_in[:, lanes].astype(F32) * skip_col

    @pl.when(is_home)
    def _():
        full, half = final.at[pl.ds(0, 31)], final.at[pl.ds(0, 32), 0]
        pltpu.make_async_copy(message.at[pl.ds(0, 63)], message.at[pl.ds(0, 63)], out_send.at[0]).wait()
        pltpu.make_async_copy(full, full, out_recv.at[0]).wait()
        pltpu.make_async_copy(half, half, out_recv.at[1]).wait()
        final[chip] = message[chip]

    @pl.when(not_home)
    def _():
        full, half = final.at[pl.ds(0, 32)], final.at[pl.ds(0, 31), 0]
        pltpu.make_async_copy(message.at[pl.ds(0, 63), 0], message.at[pl.ds(0, 63), 0], out_send.at[1]).wait()
        pltpu.make_async_copy(full, full, out_recv.at[0]).wait()
        pltpu.make_async_copy(half, half, out_recv.at[1]).wait()
        final[chip, 0] = message[chip, 0]

    conv = final[:, 0].astype(F32)
    corr = final[pl.ds(32 * chan, 32), 1].astype(F32) * (1.0 / 256.0)
    pad = jnp.zeros_like(conv)
    stage[1] = jnp.concatenate([conv, pad], axis=1).reshape(ROWS, LANES)
    for q in range(QUADS):
        lanes = slice(q * LANES, (q + 1) * LANES)
        value = stage[0, pl.ds(q, CHIPS, stride=8), :] + stage[1, pl.ds(q, CHIPS, stride=8), :]
        signal_out[:, lanes] = value.astype(BF16)
    stage[1, pl.ds(0, 256), :] = jnp.concatenate([corr, pad[:32]], axis=1).reshape(256, LANES)
    for q in range(QUADS):
        lanes = slice(q * LANES, (q + 1) * LANES)
        filter_out[:, lanes] = stage[1, pl.ds(q, 32, stride=8), :]


def local(signal, cotangent, filters, skip):
    rows_fwd, rows_inv, lanes_tab, turns = tables()
    vmem, anywhere = pl.BlockSpec(memory_space=pltpu.VMEM), pl.BlockSpec(memory_space=pl.ANY)
    dma = pltpu.SemaphoreType.DMA
    skip_row = jnp.pad(skip, (0, LANES - CHIPS)).reshape(1, LANES)
    signal_grad, filter_grad, skip_grad = pl.pallas_call(
        kernel,
        out_shape=(
            jax.ShapeDtypeStruct((CHIPS, ROWS), BF16),
            jax.ShapeDtypeStruct((CHIPS // 2, ROWS), F32),
            jax.ShapeDtypeStruct((1, LANES), F32),
        ),
        in_specs=[anywhere, anywhere, anywhere, vmem, anywhere, anywhere, anywhere, anywhere],
        out_specs=(vmem, vmem, vmem),
        scratch_shapes=[
            pltpu.VMEM((CHIPS, ROWS), BF16),
            pltpu.VMEM((CHIPS, ROWS), BF16),
            pltpu.VMEM((CHIPS, ROWS), BF16),
            pltpu.VMEM(rows_fwd.shape, BF16),
            pltpu.VMEM(rows_inv.shape, BF16),
            pltpu.VMEM(lanes_tab.shape, BF16),
            pltpu.VMEM(turns.shape, F32),
            pltpu.VMEM((2, ROWS, LANES), F32),
            pltpu.VMEM((CHIPS, 2, 8, LANES), BF16),
            pltpu.VMEM((CHIPS, 2, 8, LANES), BF16),
            pltpu.VMEM((CHIPS, 8, LANES), BF16),
            pltpu.VMEM((ROWS, 2 * LANES), BF16),
            pltpu.VMEM((2 * ROWS, 2 * LANES), BF16),
            pltpu.VMEM((CHIPS, QUADS, LANES), BF16),
            pltpu.VMEM((CHIPS, QUADS, LANES), BF16),
            pltpu.VMEM((CHIPS, QUADS, LANES), BF16),
            pltpu.VMEM((CHIPS, QUADS, LANES), BF16),
            pltpu.VMEM((CHIPS, 2, QUADS, LANES), BF16),
            pltpu.VMEM((CHIPS, 2, QUADS, LANES), BF16),
            pltpu.VMEM((8, LANES), F32),
            pltpu.VMEM((8, LANES), F32),
            pltpu.VMEM((8, 8, LANES), F32),
            pltpu.VMEM((8, LANES), F32),
            pltpu.VMEM((8, 8, LANES), F32),
            dma((3,)),
            dma((4,)),
            dma,
            dma,
            dma((2,)),
            dma((5,)),
            dma((2,)),
            dma((2,)),
            dma((3,)),
            dma((3,)),
        ],
        compiler_params=pltpu.CompilerParams(
            collective_id=0, has_side_effects=True
        ),
        name="hyena_backward",
    )(signal, cotangent, filters, skip_row, *(jnp.asarray(t) for t in (rows_fwd, rows_inv, lanes_tab, turns)))
    return signal_grad, filter_grad, skip_grad[0, :CHIPS]


def solution(mesh):
    in_specs = (P("chan", "seq"), P("chan", "seq"), P(None, "seq"), P("chan"))
    out_specs = (P("chan", "seq"), P("chan", "seq"), P("chan"))
    return jax.shard_map(local, mesh=mesh, in_specs=in_specs, out_specs=out_specs, check_vma=False)
```

time: 680 us -> 45.9 us (0.07); the launches traced: 671 us -> 45.7 us
  blocking collectives: 324 us -> 0 us
  waiting for transfers between devices: 142 us -> 0 us
  starting transfers between devices: 111 us -> 0 us
  Pallas kernels: 0 us -> 39.8 us
  matrix products: 39 us -> 0 us
  local copies, waits for them, and re-layouts: 33.6 us -> 5.29 us
  between operations: 15.7 us -> 0.64 us
    psum x1 -> x0, blocking collectives: 324 us -> none  [local(): skip_grad = lax.psum(local_skip, 'seq') * norm_factor]
    all_to_all x15 -> x0, waiting for transfers between devices: 142 us -> none  [the longest x1 12.1 us: local(): lax.all_to_all(row_spectra[1][0].astype(jnp.bfloat16), 'seq', split_axis=...]
    all_to_all x15 -> x0, starting transfers between devices: 111 us -> none  [the longest x1 16.4 us: local(): lax.all_to_all(signal.reshape(channels, 1, length), 'seq', split_axis=2,...]
    pallas_call x0 -> x1, Pallas kernels: none -> 39.8 us  [local(): pl.pallas_call(kernel, out_shape=(jax.ShapeDtypeStruct((CHIPS, ROWS), BF1...]
    dot_general x50 -> x0, matrix products: 39 us -> none  [the longest x10 7.41 us: rotate(): jnp.einsum(pattern, imag_part, sine_tab, precision=lax.Precision.HIGHEST)]
    unnamed x62 -> x2, local copies, waits for them, and re-layouts: 23.4 us -> 2.94 us
  transfers between devices with their start and end apart: 16 -> 0, of which waited for: 15 -> 0; matrix products, arithmetic and copies ran while one was open for 7% -> 0% of each run, Pallas kernels for 0% -> 0%
where the time goes in v1:
time: 45.9 us; the launch traced here: 45.7 us
  Pallas kernels  39.8 us (87%)
  local copies, waits for them, and re-layouts  5.29 us (12%)
  between operations  0.64 us (1%)
    pallas_call x1, Pallas kernels, local(): pl.pallas_call(kernel, out_shape=(jax.ShapeDtypeStruct((CHIPS, ROWS), BF1...  39.8 us
    unnamed x2, local copies, waits for them, and re-layouts  2.94 us
    squeeze x1, local copies, waits for them, and re-layouts, local(): return (signal_grad, filter_grad, skip_grad[0, :CHIPS])  1.18 us
    reshape x1, local copies, waits for them, and re-layouts, local(): skip_row = jnp.pad(skip, (0, LANES - CHIPS)).reshape(1, LANES)  1.17 us

profile of v1, /device:TPU:1, one launch (start us, length us, event | category | flops | bytes accessed | tf_op | source)
XLA Modules:
  0.0 45.7 jit_solution(14517143115673284635)
XLA Ops:
  0.6 1.2 %pad_bitcast_fusion.skip_ref = f32[1,128]{1,0:T(1,128)} fusion(f32[64]{0:T(128)} %param.11), kind=kLoop, calls=%fused_computation.1 | loop fusion | bytes 768 | tf_op jit(solution)/shard_map/reshape | solution.py:374
  1.8 39.8 %hyena_backward.1 = (bf16[64,512]{1,0:T(8,128)(2,1)}, f32[32,512]{1,0:T(8,128)}, f32[1,128]{1,0:T(1,128)}) custom-call(bf16[64,512]{1,0:T(8,128)(2,1)} %signal_hbm.1, bf16[64,512]{1,0:T(8,128)(2,1)} %cotan_hbm.1, bf16[64,512]{1,0:T(8,128)(2,1)} %filter_hbm.1, f32[1,128]{1,0:T(1,128)} %pad_bitcast_fusion.skip_ref, ...), custom_call_target="tpu_custom_call" | custom-call | tf_op jit(solution)/shard_map/hyena_backward/pallas_call | solution.py:375
  41.6 1.2 %slice_bitcast_fusion = f32[64]{0:T(128)} fusion(f32[1,128]{1,0:T(1,128)} %get-tuple-element.8), kind=kLoop, calls=%fused_computation | loop fusion | bytes 512 | tf_op jit(solution)/shard_map/squeeze | solution.py:425
  42.7 1.5 %copy.13 = bf16[64,512]{1,0:T(8,128)(2,1)} copy(bf16[64,512]{1,0:T(8,128)(2,1)} %get-tuple-element.12) | data formatting | bytes 131072
  44.2 1.5 %copy.14 = f32[32,512]{1,0:T(8,128)} copy(f32[32,512]{1,0:T(8,128)} %get-tuple-element.13) | data formatting | bytes 131072

commit v2 on v1

--- a/solution.py
+++ b/solution.py
@@ -58,12 +58,12 @@
 
 
 def kernel(
-    signal_hbm, cotan_hbm, filter_hbm, skip_ref, rows_fwd_hbm, rows_inv_hbm, lanes_hbm, turns_hbm,
-    signal_out, filter_out, skip_out,
+    signal_hbm, cotan_hbm, filter_hbm, rows_fwd_hbm, rows_inv_hbm, lanes_hbm, turns_hbm,
+    final, cross, part_line,
     signal_in, cotan_in, filter_in, rows_fwd, rows_inv, lanes_tab, turns,
-    stage, sent, got, mate, packed, spectrum, keep, give, mate_y, side_y, message, final,
-    part, part_mate, part_plane, part_plane_sum, part_line,
-    load_sem, table_sem, send_sem, recv_sem, mate_sems, back_sems, out_send, out_recv, part_send, part_recv,
+    stage, sent, got, mate, packed, spectrum, keep, give, mate_y, message,
+    part, part_mate, part_plane, part_plane_sum,
+    load_sem, table_sem, send_sem, recv_sem, mate_sems, back_sems, out_send, out_recv, part_send, part_recv, own_sem,
 ):
     me, chan = lax.axis_index("seq"), lax.axis_index("chan")
     core, chip = me % 2, me // 2
@@ -114,10 +114,14 @@
 
     lax.fori_loop(0, CHIPS - 1, greet, 0, unroll=7)
     pl.semaphore_signal(barrier, inc=1, device_id=mate_id, device_id_type=MESH)
-    for c in range(CORES):
+
+    def greet_across(i, carry):
         pl.semaphore_signal(
-            barrier, inc=1, device_id=(2 * chip + c, other_chan), device_id_type=MESH
+            barrier, inc=1, device_id=(2 * (32 * chan + i) + core, other_chan), device_id_type=MESH
         )
+        return carry
+
+    lax.fori_loop(0, CHIPS // 2, greet_across, 0, unroll=8)
 
     for load in loads:
         load.wait()
@@ -139,7 +143,7 @@
     row = jnp.sum(jnp.where(diagonal, sums, 0.0), axis=0, keepdims=True)
     part[...] = jnp.broadcast_to(row, (8, LANES))
 
-    pl.semaphore_wait(barrier, CHIPS + 2)
+    pl.semaphore_wait(barrier, CHIPS + CHIPS * not_home.astype(jnp.int32))
 
     def send(i, carry):
         to = far_first(i)
@@ -186,6 +190,8 @@
     pltpu.make_async_copy(seven, seven, part_recv.at[1]).wait()
     part_plane[spot] = part[...]
     part_plane_sum[...] = jnp.sum(part_plane[...], axis=0)
+    own_line = pltpu.make_async_copy(part_plane_sum, part_line.at[z], own_sem.at[1])
+    own_line.start()
 
     def send_line(i, carry):
         to = (z + i) % 8
@@ -240,7 +246,8 @@
             spectrum[pl.ds(k * ROWS + b * KBLOCK, KBLOCK), LANES:] = low
         return carry
 
-    lax.fori_loop(0, ROWS // KBLOCK, block, 0)
+    for b in range(ROWS // KBLOCK):
+        block(b, 0)
 
     def rows_of(parity):
         wide = dot(rows_inv[0, parity], spectrum[...])
@@ -252,48 +259,15 @@
         src_ref=give, dst_ref=mate_y, send_sem=back_sems.at[0], recv_sem=back_sems.at[1],
         device_id=mate_id, device_id_type=MESH,
     )
-    to_side_give = pltpu.make_async_remote_copy(
-        src_ref=give, dst_ref=side_y, send_sem=back_sems.at[2], recv_sem=back_sems.at[4],
-        device_id=(2 * chip + other_core, other_chan), device_id_type=MESH,
-    )
-    to_side_keep = pltpu.make_async_remote_copy(
-        src_ref=keep, dst_ref=side_y, send_sem=back_sems.at[3], recv_sem=back_sems.at[4],
-        device_id=(me, other_chan), device_id_type=MESH,
-    )
-    giver = jnp.logical_or(is_home, core == 0)
-    sider = jnp.logical_and(not_home, core == 1)
-
-    @pl.when(giver)
-    def _():
-        to_mate.start()
-
-    @pl.when(sider)
-    def _():
-        to_side_give.start()
-
+    to_mate.start()
     keep[...] = rows_of(core)
-
-    @pl.when(sider)
-    def _():
-        to_side_keep.start()
-        to_side_give.wait_send()
-        to_side_keep.wait_send()
-
-    @pl.when(giver)
-    def _():
-        to_mate.wait_send()
-
-    @pl.when(jnp.logical_or(is_home, core == 1))
-    def _():
-        to_mate.wait_recv()
+    to_mate.wait()
+    mine, others = keep[...], mate_y[...]
+    message[:, 0] = jnp.where(core == 0, mine, others)
+    message[:, 1] = jnp.where(core == 0, others, mine)
 
     @pl.when(is_home)
     def _():
-        to_side_keep.wait_recv()
-        mine, others = keep[...].astype(F32), mate_y[...].astype(F32)
-        message[:, 0] = jnp.where(core == 0, mine, others).astype(BF16)
-        message[:, 1] = (jnp.where(core == 0, others, mine) + side_y[...].astype(F32)).astype(BF16)
-
         def send_back(i, carry):
             to = far_first(i)
             pltpu.make_async_remote_copy(
@@ -304,18 +278,17 @@
 
         lax.fori_loop(0, CHIPS - 1, send_back, 0, unroll=7)
 
-    @pl.when(jnp.logical_and(not_home, core == 0))
-    def _():
-        message[:, 0] = keep[...]
-
-    @pl.when(jnp.logical_and(not_home, core == 1))
-    def _():
-        message[:, 0] = mate_y[...]
-
     @pl.when(not_home)
     def _():
+        def send_across(to):
+            pltpu.make_async_remote_copy(
+                src_ref=message.at[to, 1], dst_ref=cross.at[chip % 32], send_sem=out_send.at[2], recv_sem=out_recv.at[2],
+                device_id=(2 * to + core, other_chan), device_id_type=MESH,
+            ).start()
+
         def send_back(i, carry):
             to = far_first(i)
+            send_across(to)
             pltpu.make_async_remote_copy(
                 src_ref=message.at[to, 0], dst_ref=final.at[chip, 0], send_sem=out_send.at[1], recv_sem=out_recv.at[1],
                 device_id=device(to), device_id_type=MESH,
@@ -323,19 +296,17 @@
             return carry
 
         lax.fori_loop(0, CHIPS - 1, send_back, 0, unroll=7)
-
+        send_across(chip)
+
+    own_rows = pltpu.make_async_copy(message.at[chip], final.at[chip], own_sem.at[0])
+    own_rows.start()
     line = part_line.at[pl.ds(0, 7)]
     pltpu.make_async_copy(line, line, part_send.at[2]).wait()
     pltpu.make_async_copy(line, line, part_recv.at[2]).wait()
-    part_line[z] = part_plane_sum[...]
-    skip_out[...] = jnp.sum(part_line[...], axis=0)[:1] * (1.0 / 256.0)
-
-    skip_col = jnp.sum(
-        jnp.where(diagonal, jnp.broadcast_to(skip_ref[...], (CHIPS, LANES)), 0.0), axis=1, keepdims=True
-    )
-    for q in range(QUADS):
-        lanes = slice(q * LANES, (q + 1) * LANES)
-        stage[0, pl.ds(q, CHIPS, stride=8), :] = cotan_in[:, lanes].astype(F32) * skip_col
+    own_line.wait()
+    own_rows.wait()
+    across = cross.at[pl.ds(0, 32)]
+    pltpu.make_async_copy(across, across, out_recv.at[2]).wait()
 
     @pl.when(is_home)
     def _():
@@ -343,44 +314,44 @@
         pltpu.make_async_copy(message.at[pl.ds(0, 63)], message.at[pl.ds(0, 63)], out_send.at[0]).wait()
         pltpu.make_async_copy(full, full, out_recv.at[0]).wait()
         pltpu.make_async_copy(half, half, out_recv.at[1]).wait()
-        final[chip] = message[chip]
 
     @pl.when(not_home)
     def _():
         full, half = final.at[pl.ds(0, 32)], final.at[pl.ds(0, 31), 0]
         pltpu.make_async_copy(message.at[pl.ds(0, 63), 0], message.at[pl.ds(0, 63), 0], out_send.at[1]).wait()
+        pltpu.make_async_copy(message.at[:, 0], message.at[:, 0], out_send.at[2]).wait()
         pltpu.make_async_copy(full, full, out_recv.at[0]).wait()
         pltpu.make_async_copy(half, half, out_recv.at[1]).wait()
-        final[chip, 0] = message[chip, 0]
-
+
+
+def finish(final, cross, part_line, cotan, skip_ref, signal_out, filter_out, skip_out, stage):
+    chan = lax.axis_index("chan")
+    row, column = (lax.broadcasted_iota(jnp.int32, (CHIPS, CHIPS), d) for d in range(2))
+    skip_col = jnp.sum(jnp.where(row == column, skip_ref[...], 0.0), axis=1, keepdims=True)
     conv = final[:, 0].astype(F32)
-    corr = final[pl.ds(32 * chan, 32), 1].astype(F32) * (1.0 / 256.0)
-    pad = jnp.zeros_like(conv)
-    stage[1] = jnp.concatenate([conv, pad], axis=1).reshape(ROWS, LANES)
+    corr = final[pl.ds(32 * chan, 32), 1].astype(F32) + cross[...].astype(F32)
+    stage[...] = jnp.concatenate([conv, jnp.concatenate([corr, corr], axis=0)], axis=1).reshape(ROWS, LANES)
     for q in range(QUADS):
         lanes = slice(q * LANES, (q + 1) * LANES)
-        value = stage[0, pl.ds(q, CHIPS, stride=8), :] + stage[1, pl.ds(q, CHIPS, stride=8), :]
-        signal_out[:, lanes] = value.astype(BF16)
-    stage[1, pl.ds(0, 256), :] = jnp.concatenate([corr, pad[:32]], axis=1).reshape(256, LANES)
-    for q in range(QUADS):
-        lanes = slice(q * LANES, (q + 1) * LANES)
-        filter_out[:, lanes] = stage[1, pl.ds(q, 32, stride=8), :]
+        conv_rows = stage[pl.ds(q, CHIPS, stride=8), :]
+        signal_out[:, lanes] = (conv_rows + cotan[:, lanes].astype(F32) * skip_col).astype(BF16)
+        filter_out[:, lanes] = stage[pl.ds(4 + q, 32, stride=8), :] * (1.0 / 256.0)
+    skip_out[...] = jnp.sum(part_line[...], axis=0)[:1, :CHIPS] * (1.0 / 256.0)
 
 
 def local(signal, cotangent, filters, skip):
     rows_fwd, rows_inv, lanes_tab, turns = tables()
     vmem, anywhere = pl.BlockSpec(memory_space=pltpu.VMEM), pl.BlockSpec(memory_space=pl.ANY)
     dma = pltpu.SemaphoreType.DMA
-    skip_row = jnp.pad(skip, (0, LANES - CHIPS)).reshape(1, LANES)
-    signal_grad, filter_grad, skip_grad = pl.pallas_call(
+    final, cross, part_line = pl.pallas_call(
         kernel,
         out_shape=(
-            jax.ShapeDtypeStruct((CHIPS, ROWS), BF16),
-            jax.ShapeDtypeStruct((CHIPS // 2, ROWS), F32),
-            jax.ShapeDtypeStruct((1, LANES), F32),
+            jax.ShapeDtypeStruct((CHIPS, 2, QUADS, LANES), BF16),
+            jax.ShapeDtypeStruct((CHIPS // 2, QUADS, LANES), BF16),
+            jax.ShapeDtypeStruct((8, 8, LANES), F32),
         ),
-        in_specs=[anywhere, anywhere, anywhere, vmem, anywhere, anywhere, anywhere, anywhere],
-        out_specs=(vmem, vmem, vmem),
+        in_specs=[anywhere] * 7,
+        out_specs=(anywhere,) * 3,
         scratch_shapes=[
             pltpu.VMEM((CHIPS, ROWS), BF16),
             pltpu.VMEM((CHIPS, ROWS), BF16),
@@ -398,31 +369,41 @@
             pltpu.VMEM((CHIPS, QUADS, LANES), BF16),
             pltpu.VMEM((CHIPS, QUADS, LANES), BF16),
             pltpu.VMEM((CHIPS, QUADS, LANES), BF16),
-            pltpu.VMEM((CHIPS, QUADS, LANES), BF16),
-            pltpu.VMEM((CHIPS, 2, QUADS, LANES), BF16),
             pltpu.VMEM((CHIPS, 2, QUADS, LANES), BF16),
             pltpu.VMEM((8, LANES), F32),
             pltpu.VMEM((8, LANES), F32),
             pltpu.VMEM((8, 8, LANES), F32),
             pltpu.VMEM((8, LANES), F32),
-            pltpu.VMEM((8, 8, LANES), F32),
             dma((3,)),
             dma((4,)),
             dma,
             dma,
             dma((2,)),
-            dma((5,)),
-            dma((2,)),
             dma((2,)),
             dma((3,)),
             dma((3,)),
+            dma((3,)),
+            dma((3,)),
+            dma((2,)),
         ],
         compiler_params=pltpu.CompilerParams(
             collective_id=0, has_side_effects=True
         ),
         name="hyena_backward",
-    )(signal, cotangent, filters, skip_row, *(jnp.asarray(t) for t in (rows_fwd, rows_inv, lanes_tab, turns)))
-    return signal_grad, filter_grad, skip_grad[0, :CHIPS]
+    )(signal, cotangent, filters, *(jnp.asarray(t) for t in (rows_fwd, rows_inv, lanes_tab, turns)))
+    signal_grad, filter_grad, skip_grad = pl.pallas_call(
+        finish,
+        out_shape=(
+            jax.ShapeDtypeStruct((CHIPS, ROWS), BF16),
+            jax.ShapeDtypeStruct((CHIPS // 2, ROWS), F32),
+            jax.ShapeDtypeStruct((1, CHIPS), F32),
+        ),
+        in_specs=[vmem] * 5,
+        out_specs=(vmem,) * 3,
+        scratch_shapes=[pltpu.VMEM((ROWS, LANES), F32)],
+        name="finish",
+    )(final, cross, part_line, cotangent, skip.reshape(1, CHIPS))
+    return signal_grad, filter_grad, skip_grad.reshape(CHIPS)
 
 
 def solution(mesh):

time: 45.9 us -> 39.6 us (0.86)
  local copies, waits for them, and re-layouts: 5.29 us -> 0 us
  Pallas kernels: 39.8 us -> 38.9 us
    unnamed x2 -> x0, local copies, waits for them, and re-layouts: 2.94 us -> none
    squeeze x1 -> x0, local copies, waits for them, and re-layouts: 1.18 us -> none  [local(): return (signal_grad, filter_grad, skip_grad[0, :CHIPS])]
    reshape x1 -> x0, local copies, waits for them, and re-layouts: 1.17 us -> none  [local(): skip_row = jnp.pad(skip, (0, LANES - CHIPS)).reshape(1, LANES)]
    pallas_call x1 -> x2, Pallas kernels: 39.8 us -> 38.9 us  [the longest x1 37.2 us: local(): pl.pallas_call(kernel, out_shape=(jax.ShapeDtypeStruct((CHIPS, 2, QUADS,...]
where the time goes in v2:
time: 39.6 us; the launch traced here: 39.5 us
  Pallas kernels  38.9 us (98%)
  between operations  0.64 us (2%)
    pallas_call x1, Pallas kernels, local(): pl.pallas_call(kernel, out_shape=(jax.ShapeDtypeStruct((CHIPS, 2, QUADS,...  37.2 us
    pallas_call x1, Pallas kernels, local(): pl.pallas_call(finish, out_shape=(jax.ShapeDtypeStruct((CHIPS, ROWS), BF1...  1.7 us

profile of v2, /device:TPU:1, one launch (start us, length us, event | category | flops | bytes accessed | tf_op | source)
XLA Modules:
  0.0 39.5 jit_solution(13633084945295870118)
XLA Ops:
  0.6 37.2 %hyena_backward.1 = (bf16[64,2,4,128]{3,2,1,0:T(4,128)(2,1)}, bf16[32,4,128]{2,1,0:T(4,128)(2,1)}, f32[8,8,128]{2,1,0:T(8,128)}) custom-call(bf16[64,512]{1,0:T(8,128)(2,1)} %signal_hbm.1, bf16[64,512]{1,0:T(8,128)(2,1)} %cotan.1, bf16[64,512]{1,0:T(8,128)(2,1)} %filter_hbm.1, bf16[2,2,512,512]{3,2,1,0:T(8,128)(2,1)} %constant.8.clone.rows_fwd_hbm, ...), custom_call_target="tpu_custom_call" | custom-call | tf_op jit(solution)/shard_map/hyena_backward/pallas_call | solution.py:346
  37.9 1.7 %finish.1 = (bf16[64,512]{1,0:T(8,128)(2,1)}, f32[32,512]{1,0:T(8,128)}, f32[1,64]{1,0:T(1,128)}) custom-call(bf16[64,2,4,128]{3,2,1,0:T(4,128)(2,1)} %get-tuple-element.9.final, bf16[32,4,128]{2,1,0:T(4,128)(2,1)} %get-tuple-element.10.cross, f32[8,8,128]{2,1,0:T(8,128)} %get-tuple-element.11.part_line, bf16[64,512]{1,0:T(8,128)(2,1)} %cotan.1, f32[1,64]{1,0:T(1,128)} %bitcast.2), custom_call_target="tpu_custom_call" | custom-call | tf_op jit(solution)/shard_map/finish/pallas_call | solution.py:394

commit v3 on v2

v3 whole, which is shorter than its diff:
```python
import functools
import math

import jax
import jax.numpy as jnp
import ml_dtypes
import numpy as np
from jax import lax
from jax.experimental import pallas as pl
from jax.experimental.pallas import tpu as pltpu
from jax.sharding import PartitionSpec as P

MESH = pl.DeviceIdType.MESH
F32, BF16 = jnp.float32, jnp.bfloat16
CHIPS, CORES, LANES, ROWS, QUADS = 64, 2, 128, 512, 4
KBLOCK = 256


def high_low(table):
    high = table.astype(ml_dtypes.bfloat16)
    low = (table - high.astype(np.float64)).astype(ml_dtypes.bfloat16)
    return np.stack([high, low])


@functools.lru_cache(None)
def tables():
    k1 = np.arange(ROWS)
    row_angle = np.pi * ((2 * k1[:, None] + 1) * np.arange(ROWS)[None, :] % 2048) / 1024.0
    blocks = ROWS // KBLOCK
    cos_rows = np.cos(row_angle).reshape(blocks, KBLOCK, ROWS)
    sin_rows = np.sin(row_angle).reshape(blocks, KBLOCK, ROWS)
    rows_fwd = high_low(np.concatenate([cos_rows, -sin_rows], axis=1))
    back = np.concatenate([np.cos(row_angle).T, -np.sin(row_angle).T], axis=1)
    rows_inv = high_low(back.reshape(2, ROWS // 2, 2 * ROWS))
    lane = np.arange(LANES)
    lane_angle = 2.0 * np.pi * (lane[:, None] * lane[None, :] % LANES) / LANES
    cos, sin = np.cos(lane_angle), np.sin(lane_angle)
    lanes_fwd = high_low(np.block([[cos, -sin], [sin, cos]]))
    lanes_inv = high_low(np.block([[cos, sin], [-sin, cos]]))
    turn = np.pi * (2 * k1[:, None] + 1) * lane[None, :] / 131072.0
    turns = np.stack([np.cos(turn), np.sin(turn)]).astype(np.float32)
    return rows_fwd, rows_inv, np.stack([lanes_fwd, lanes_inv]), turns


def split(x):
    high = x.astype(BF16)
    return high, (x - high.astype(F32)).astype(BF16)


def dot(a, b):
    return jnp.dot(a, b, preferred_element_type=F32)


def three_pass(x, high, low):
    x_high, x_low = split(x)
    return dot(x_high, high) + dot(x_low, high) + dot(x_high, low)


def kernel(
    signal_hbm, cotan_hbm, filter_hbm, rows_fwd_hbm, rows_inv_hbm, lanes_hbm, turns_hbm,
    conv, corr, part_line,
    signal_in, cotan_in, filter_in, rows_fwd, rows_inv, lanes_tab, turns,
    stage, sent, got, mate, packed, spectrum, result,
    part, part_mate, part_plane, part_plane_sum,
    load_sem, table_sem, send_sem, recv_sem, mate_sems, out_send, conv_recv, corr_recv, part_send, part_recv, own_sem, cross_sem,
):
    me, chan = lax.axis_index("seq"), lax.axis_index("chan")
    core, chip = me % 2, me // 2
    other_core, other_chan = 1 - core, 1 - chan
    z, y, x = chip // 8, (chip // 2) % 4, chip % 2
    home = chip // 32
    is_home, not_home = home == chan, home != chan
    plane_order = [(2, 1), (1, 1), (3, 1), (2, 0), (0, 1), (1, 0), (3, 0), (0, 0)]

    def in_plane(z_to, dy, dx):
        return (z_to * 4 + (y + dy) % 4) * 2 + (x + dx) % 2

    def each_chip(visit):
        def plane(k, carry):
            z_to = (z + 4 + (1 - 2 * (k % 2)) * ((k + 1) // 2)) % 8
            for dy, dx in plane_order:
                visit(in_plane(z_to, dy, dx))
            return carry

        lax.fori_loop(0, 7, plane, 0)
        for dy, dx in plane_order[:-1]:
            visit(in_plane(z, dy, dx))

    mate_id = (2 * chip + other_core, chan)
    barrier = pltpu.get_barrier_semaphore()

    def greet(to):
        pl.semaphore_signal(barrier, inc=1, device_id=(2 * to + core, chan), device_id_type=MESH)

    each_chip(greet)
    pl.semaphore_signal(barrier, inc=1, device_id=mate_id, device_id_type=MESH)
    for c in range(CORES):
        pl.semaphore_signal(barrier, inc=1, device_id=(2 * chip + c, other_chan), device_id_type=MESH)

    def load_all(pairs, sem):
        copies = [pltpu.make_async_copy(src, dst, sem.at[i]) for i, (src, dst) in enumerate(pairs)]
        for copy in copies:
            copy.start()
        return copies

    loads = load_all(
        ((signal_hbm, signal_in), (cotan_hbm, cotan_in), (filter_hbm, filter_in)), load_sem
    )
    table_loads = load_all(
        ((rows_fwd_hbm, rows_fwd), (rows_inv_hbm, rows_inv), (lanes_hbm, lanes_tab), (turns_hbm, turns)),
        table_sem,
    )

    values = []
    for k, (load, ref) in enumerate(zip(loads, (signal_in, cotan_in, filter_in))):
        load.wait()
        value = ref[...].astype(F32)
        values.append(value)
        for q in range(QUADS):
            stage[k, pl.ds(q, CHIPS, stride=QUADS), :] = value[:, q * LANES : (q + 1) * LANES]
        sent[:, k] = stage[k].reshape(CHIPS, QUADS, LANES).astype(BF16)
    sums = jnp.sum(values[0] * values[1], axis=1, keepdims=True)
    diagonal = lax.broadcasted_iota(jnp.int32, (CHIPS, LANES), 0) == lax.broadcasted_iota(
        jnp.int32, (CHIPS, LANES), 1
    )
    row = jnp.sum(jnp.where(diagonal, sums, 0.0), axis=0, keepdims=True)
    part[...] = jnp.broadcast_to(row, (8, LANES))

    pl.semaphore_wait(barrier, CHIPS + 2)

    def send(to):
        pltpu.make_async_remote_copy(
            src_ref=sent.at[to], dst_ref=got.at[chip], send_sem=send_sem, recv_sem=recv_sem,
            device_id=(2 * to + core, chan), device_id_type=MESH,
        ).start()

    each_chip(send)
    got[chip] = sent[chip]

    @pl.when(is_home)
    def _():
        pl.semaphore_signal(cross_sem, inc=1, device_id=(2 * chip + 1, other_chan), device_id_type=MESH)

    mate_part = pltpu.make_async_remote_copy(
        src_ref=part, dst_ref=part_mate, send_sem=part_send.at[0], recv_sem=part_recv.at[0],
        device_id=mate_id, device_id_type=MESH,
    )
    mate_part.start()
    mate_part.wait()
    part[...] = part[...] + part_mate[...]
    spot = chip % 8

    def send_plane(i, carry):
        pltpu.make_async_remote_copy(
            src_ref=part, dst_ref=part_plane.at[spot], send_sem=part_send.at[1], recv_sem=part_recv.at[1],
            device_id=(2 * (chip // 8 * 8 + (spot + i) % 8) + core, chan), device_id_type=MESH,
        ).start()
        return carry

    lax.fori_loop(1, 8, send_plane, 0)

    all_but_one = got.at[pl.ds(0, CHIPS - 1)]
    pltpu.make_async_copy(all_but_one, all_but_one, recv_sem).wait()

    swap = pltpu.make_async_remote_copy(
        src_ref=got.at[:, pl.ds(core, 2)], dst_ref=mate, send_sem=mate_sems.at[0], recv_sem=mate_sems.at[1],
        device_id=mate_id, device_id_type=MESH,
    )
    swap.start()

    pltpu.make_async_copy(all_but_one, all_but_one, send_sem).wait()
    seven = part_plane.at[pl.ds(0, 7)]
    pltpu.make_async_copy(seven, seven, part_send.at[1]).wait()
    pltpu.make_async_copy(seven, seven, part_recv.at[1]).wait()
    part_plane[spot] = part[...]
    part_plane_sum[...] = jnp.sum(part_plane[...], axis=0)

    def send_line(i, carry):
        pltpu.make_async_remote_copy(
            src_ref=part_plane_sum, dst_ref=part_line.at[z], send_sem=part_send.at[2], recv_sem=part_recv.at[2],
            device_id=(2 * ((z + i) % 8 * 8 + spot) + core, chan), device_id_type=MESH,
        ).start()
        return carry

    lax.fori_loop(1, 8, send_line, 0)
    own_line = pltpu.make_async_copy(part_plane_sum, part_line.at[z], own_sem.at[1])
    own_line.start()
    for load in table_loads:
        load.wait()
    swap.wait()

    for k, (ours, theirs) in enumerate(((2 - 2 * core, other_core), (1, core))):
        ours, theirs = got[:, ours].astype(F32), mate[:, theirs].astype(F32)
        first = jnp.where(core == 0, ours, theirs)
        second = jnp.where(core == 0, theirs, ours)
        both = jnp.concatenate([first, second], axis=1)
        packed[:, k * LANES : (k + 1) * LANES] = both.reshape(ROWS, LANES).astype(BF16)

    def block(b, carry):
        span = pl.ds(b * KBLOCK, KBLOCK)
        cos, sin = turns[0, span, :], turns[1, span, :]
        right = packed[...]
        waves = dot(rows_fwd[0, b], right) + dot(rows_fwd[1, b], right)
        real, imag = waves[:KBLOCK], waves[KBLOCK:]
        cos2 = jnp.concatenate([cos, cos], axis=1)
        sin2 = jnp.concatenate([sin, sin], axis=1)
        real, imag = real * cos2 + imag * sin2, imag * cos2 - real * sin2
        left = jnp.concatenate(
            [
                jnp.concatenate([real[:, :LANES], imag[:, :LANES]], axis=1),
                jnp.concatenate([real[:, LANES:], imag[:, LANES:]], axis=1),
            ],
            axis=0,
        )
        freq = three_pass(left, lanes_tab[0, 0], lanes_tab[0, 1])
        b_real, b_imag = freq[:KBLOCK, :LANES], freq[:KBLOCK, LANES:]
        g_real, g_imag = freq[KBLOCK:, :LANES], freq[KBLOCK:, LANES:]
        product = jnp.concatenate(
            [b_real * g_real + b_imag * g_imag, b_real * g_imag - b_imag * g_real], axis=1
        )
        inner = three_pass(product, lanes_tab[1, 0], lanes_tab[1, 1])
        real, imag = inner[:, :LANES], inner[:, LANES:]
        real, imag = real * cos - imag * sin, imag * cos + real * sin
        for k, value in enumerate((real, imag)):
            high, low = split(value)
            spectrum[pl.ds(k * ROWS + b * KBLOCK, KBLOCK), :LANES] = high
            spectrum[pl.ds(k * ROWS + b * KBLOCK, KBLOCK), LANES:] = low
        return carry

    for b in range(ROWS // KBLOCK):
        block(b, 0)

    def rows_of(half):
        wide = dot(rows_inv[0, half], spectrum[...])
        value = wide[:, :LANES] + wide[:, LANES:] + dot(rows_inv[1, half], spectrum[:, :LANES])
        result[pl.ds(32 * half, 32)] = (value * (2.0 / 131072.0)).reshape(CHIPS // 2, CORES, QUADS, LANES).astype(BF16)

    def send_conv(to, c):
        pltpu.make_async_remote_copy(
            src_ref=result.at[to, c], dst_ref=conv.at[chip], send_sem=out_send, recv_sem=conv_recv,
            device_id=(2 * to + c, chan), device_id_type=MESH,
        ).start()

    side = (home + chan) % 2

    def send_corr(to, c):
        pltpu.make_async_remote_copy(
            src_ref=result.at[to, c], dst_ref=corr.at[side, chip % 32], send_sem=out_send, recv_sem=corr_recv.at[side],
            device_id=(2 * to + c, home), device_id_type=MESH,
        ).start()

    own_conv = pltpu.make_async_copy(result.at[chip, core], conv.at[chip], own_sem.at[0])
    own_corr = pltpu.make_async_copy(result.at[chip, core], corr.at[0, chip % 32], own_sem.at[0])

    def send_half(half, order, send_to):
        for k, step in enumerate(order):
            z_to = 4 * half + (z + step) % 4
            for dy, dx in plane_order:
                to = in_plane(z_to, dy, dx)
                send_to(to, other_core)
                if step or (dy, dx) != (0, 0) or k == 0:
                    send_to(to, core)

    far_half, near_half = 1 - z // 4, z // 4
    far_order, near_order = (0, 1, 3, 2), (2, 1, 3, 0)
    rows_of(far_half)

    @pl.when(core == 0)
    def _():
        send_half(far_half, far_order, send_conv)

    @pl.when(jnp.logical_and(core == 1, not_home))
    def _():
        pl.semaphore_wait(cross_sem, 2)

    @pl.when(core == 1)
    def _():
        send_half(far_half, far_order, send_corr)

    rows_of(near_half)

    @pl.when(core == 0)
    def _():
        send_half(near_half, near_order, send_conv)
        own_conv.start()
        own_conv.wait()

    @pl.when(core == 1)
    def _():
        send_half(near_half, near_order, send_corr)

    @pl.when(jnp.logical_and(core == 1, is_home))
    def _():
        own_corr.start()
        own_corr.wait()

    @pl.when(jnp.logical_and(core == 1, not_home))
    def _():
        send_corr(chip, core)

    own_line.wait()
    line = part_line.at[pl.ds(0, 7)]
    pltpu.make_async_copy(line, line, part_send.at[2]).wait()
    pltpu.make_async_copy(line, line, part_recv.at[2]).wait()
    for c, whole, short, sem in (
        (0, conv, conv.at[pl.ds(0, 63)], conv_recv),
        (1, corr.at[0], corr.at[0, pl.ds(0, 31)], corr_recv.at[0]),
    ):
        keeps_own = core == 0 if c == 0 else jnp.logical_and(core == 1, is_home)

        @pl.when(keeps_own)
        def _():
            pltpu.make_async_copy(short, short, sem).wait()

        @pl.when(jnp.logical_not(keeps_own))
        def _():
            pltpu.make_async_copy(whole, whole, sem).wait()

    pltpu.make_async_copy(corr.at[1], corr.at[1], corr_recv.at[1]).wait()
    most = result.at[pl.ds(0, 63)]
    pltpu.make_async_copy(most, most, out_send).wait()
    pltpu.make_async_copy(result.at[0, 0], result.at[0, 0], out_send).wait()

    @pl.when(jnp.logical_and(core == 1, not_home))
    def _():
        pltpu.make_async_copy(result.at[0, 0], result.at[0, 0], out_send).wait()


def finish(conv, corr, part_line, cotan, skip_ref, signal_out, filter_out, skip_out, stage):
    row, column = (lax.broadcasted_iota(jnp.int32, (CHIPS, CHIPS), d) for d in range(2))
    skip_col = jnp.sum(jnp.where(row == column, skip_ref[...], 0.0), axis=1, keepdims=True)
    stage[0] = conv[...].astype(F32).reshape(CHIPS * QUADS, LANES)
    both = corr[0].astype(F32) + corr[1].astype(F32)
    stage[1, pl.ds(0, 32 * QUADS), :] = both.reshape(32 * QUADS, LANES)
    for q in range(QUADS):
        lanes = slice(q * LANES, (q + 1) * LANES)
        conv_rows = stage[0, pl.ds(q, CHIPS, stride=QUADS), :]
        signal_out[:, lanes] = (conv_rows + cotan[:, lanes].astype(F32) * skip_col).astype(BF16)
        filter_out[:, lanes] = stage[1, pl.ds(q, 32, stride=QUADS), :] * (1.0 / 256.0)
    skip_out[...] = jnp.sum(part_line[...], axis=0)[:1, :CHIPS] * (1.0 / 256.0)


def local(signal, cotangent, filters, skip):
    rows_fwd, rows_inv, lanes_tab, turns = tables()
    vmem, anywhere = pl.BlockSpec(memory_space=pltpu.VMEM), pl.BlockSpec(memory_space=pl.ANY)
    dma = pltpu.SemaphoreType.DMA
    conv, corr, part_line = pl.pallas_call(
        kernel,
        out_shape=(
            pltpu.VMEM((CHIPS, QUADS, LANES), BF16),
            pltpu.VMEM((2, CHIPS // 2, QUADS, LANES), BF16),
            pltpu.VMEM((8, 8, LANES), F32),
        ),
        in_specs=[anywhere] * 7,
        out_specs=(vmem,) * 3,
        scratch_shapes=[
            pltpu.VMEM((CHIPS, ROWS), BF16),
            pltpu.VMEM((CHIPS, ROWS), BF16),
            pltpu.VMEM((CHIPS, ROWS), BF16),
            pltpu.VMEM(rows_fwd.shape, BF16),
            pltpu.VMEM(rows_inv.shape, BF16),
            pltpu.VMEM(lanes_tab.shape, BF16),
            pltpu.VMEM(turns.shape, F32),
            pltpu.VMEM((3, CHIPS * QUADS, LANES), F32),
            pltpu.VMEM((CHIPS, 3, QUADS, LANES), BF16),
            pltpu.VMEM((CHIPS, 3, QUADS, LANES), BF16),
            pltpu.VMEM((CHIPS, 2, QUADS, LANES), BF16),
            pltpu.VMEM((ROWS, 2 * LANES), BF16),
            pltpu.VMEM((2 * ROWS, 2 * LANES), BF16),
            pltpu.VMEM((CHIPS, CORES, QUADS, LANES), BF16),
            pltpu.VMEM((8, LANES), F32),
            pltpu.VMEM((8, LANES), F32),
            pltpu.VMEM((8, 8, LANES), F32),
            pltpu.VMEM((8, LANES), F32),
            dma((3,)),
            dma((4,)),
            dma,
            dma,
            dma((2,)),
            dma,
            dma,
            dma((2,)),
            dma((3,)),
            dma((3,)),
            dma((2,)),
            pltpu.SemaphoreType.REGULAR,
        ],
        compiler_params=pltpu.CompilerParams(collective_id=0, has_side_effects=True),
        name="hyena_backward",
    )(signal, cotangent, filters, *(jnp.asarray(t) for t in (rows_fwd, rows_inv, lanes_tab, turns)))
    signal_grad, filter_grad, skip_grad = pl.pallas_call(
        finish,
        out_shape=(
            jax.ShapeDtypeStruct((CHIPS, ROWS), BF16),
            jax.ShapeDtypeStruct((CHIPS // 2, ROWS), F32),
            jax.ShapeDtypeStruct((1, CHIPS), F32),
        ),
        in_specs=[vmem] * 5,
        out_specs=(vmem,) * 3,
        scratch_shapes=[pltpu.VMEM((2, CHIPS * QUADS, LANES), F32)],
        name="finish",
        compiler_params=pltpu.CompilerParams(vmem_limit_bytes=8 * 1024 * 1024),
    )(*(pltpu.with_memory_space_constraint(v, pltpu.VMEM) for v in (conv, corr, part_line)), cotangent, skip.reshape(1, CHIPS))
    return signal_grad, filter_grad, skip_grad.reshape(CHIPS)


def solution(mesh):
    in_specs = (P("chan", "seq"), P("chan", "seq"), P(None, "seq"), P("chan"))
    out_specs = (P("chan", "seq"), P("chan", "seq"), P("chan"))
    return jax.shard_map(local, mesh=mesh, in_specs=in_specs, out_specs=out_specs, check_vma=False)
```

time: 39.6 us -> 34.5 us (0.87)
  Pallas kernels: 38.9 us -> 33.7 us
    pallas_call x1, Pallas kernels: 37.2 us -> 33 us  [local(): pl.pallas_call(kernel, out_shape=(pltpu.VMEM((CHIPS, QUADS, LANES), BF16)...]
    pallas_call x1, Pallas kernels: 1.7 us -> 0.73 us  [local(): pl.pallas_call(finish, out_shape=(jax.ShapeDtypeStruct((CHIPS, ROWS), BF1...]
where the time goes in v3:
time: 34.5 us; the launch traced here: 34.4 us
  Pallas kernels  33.7 us (98%)
  between operations  0.67 us (2%)
    pallas_call x1, Pallas kernels, local(): pl.pallas_call(kernel, out_shape=(pltpu.VMEM((CHIPS, QUADS, LANES), BF16)...  33 us
    pallas_call x1, Pallas kernels, local(): pl.pallas_call(finish, out_shape=(jax.ShapeDtypeStruct((CHIPS, ROWS), BF1...  0.73 us

profile of v3, /device:TPU:1, one launch (start us, length us, event | category | flops | bytes accessed | tf_op | source)
XLA Modules:
  0.0 34.4 jit_solution(17010765725793555737)
XLA Ops:
  0.6 0.0 copy-start
  0.6 0.0 copy-start.1
  0.7 33.0 %hyena_backward.1 = (bf16[64,4,128]{2,1,0:T(4,128)(2,1)S(1)}, bf16[2,32,4,128]{3,2,1,0:T(4,128)(2,1)S(1)}, f32[8,8,128]{2,1,0:T(8,128)S(1)}) custom-call(bf16[64,512]{1,0:T(8,128)(2,1)} %signal_hbm.1, bf16[64,512]{1,0:T(8,128)(2,1)} %cotan.1, bf16[64,512]{1,0:T(8,128)(2,1)} %filter_hbm.1, bf16[2,2,512,512]{3,2,1,0:T(8,128)(2,1)} %constant.8.clone.rows_fwd_hbm, ...), custom_call_target="tpu_custom_call" | custom-call | tf_op jit(solution)/shard_map/hyena_backward/pallas_call | solution.py:347
  33.7 0.0 copy-done
  33.7 0.0 copy-done.1
  33.7 0.7 %finish.1 = (bf16[64,512]{1,0:T(8,128)(2,1)}, f32[32,512]{1,0:T(8,128)}, f32[1,64]{1,0:T(1,128)}) custom-call(bf16[64,4,128]{2,1,0:T(4,128)(2,1)S(1)} %get-tuple-element.9.conv, bf16[2,32,4,128]{3,2,1,0:T(4,128)(2,1)S(1)} %get-tuple-element.10.corr, f32[8,8,128]{2,1,0:T(8,128)S(1)} %get-tuple-element.11.part_line, bf16[64,512]{1,0:T(8,128)(2,1)S(1)} %copy-done, ...), custom_call_target="tpu_custom_call" | custom-call | tf_op jit(solution)/shard_map/finish/pallas_call | solution.py:391
Async XLA Ops:
  0.6 33.0 %copy-start = (bf16[64,512]{1,0:T(8,128)(2,1)S(1)}, bf16[64,512]{1,0:T(8,128)(2,1)}, u32[]{:S(2)}) copy-start(bf16[64,512]{1,0:T(8,128)(2,1)} %cotan.1) | copy-start | bytes 196612
  0.6 33.0 %copy-start.1 = (f32[64]{0:T(128)S(1)}, f32[64]{0:T(128)}, u32[]{:S(2)}) copy-start(f32[64]{0:T(128)} %param.11) | copy-start | bytes 772

commit v4 on v3

--- a/solution.py
+++ b/solution.py
@@ -13,7 +13,8 @@
 MESH = pl.DeviceIdType.MESH
 F32, BF16 = jnp.float32, jnp.bfloat16
 CHIPS, CORES, LANES, ROWS, QUADS = 64, 2, 128, 512, 4
-KBLOCK = 256
+HALF = 256
+GROUPS = ((0, 2, 4, 6), (1, 3, 5, 7))
 
 
 def high_low(table):
@@ -24,20 +25,19 @@
 
 @functools.lru_cache(None)
 def tables():
-    k1 = np.arange(ROWS)
-    row_angle = np.pi * ((2 * k1[:, None] + 1) * np.arange(ROWS)[None, :] % 2048) / 1024.0
-    blocks = ROWS // KBLOCK
-    cos_rows = np.cos(row_angle).reshape(blocks, KBLOCK, ROWS)
-    sin_rows = np.sin(row_angle).reshape(blocks, KBLOCK, ROWS)
-    rows_fwd = high_low(np.concatenate([cos_rows, -sin_rows], axis=1))
-    back = np.concatenate([np.cos(row_angle).T, -np.sin(row_angle).T], axis=1)
-    rows_inv = high_low(back.reshape(2, ROWS // 2, 2 * ROWS))
+    k1 = np.arange(HALF)
+    rows = np.stack([(8 * np.arange(CHIPS)[None, :] + np.array(group)[:, None]).reshape(-1) for group in GROUPS])
+    angle = np.pi * ((2 * k1[None, :, None] + 1) * rows[:, None, :] % 2048) / 1024.0
+    rows_fwd = high_low(np.concatenate([np.cos(angle), -np.sin(angle)], axis=1))
+    back = angle.transpose(0, 2, 1)
+    rows_inv = high_low(np.concatenate([np.cos(back), -np.sin(back)], axis=2))
     lane = np.arange(LANES)
     lane_angle = 2.0 * np.pi * (lane[:, None] * lane[None, :] % LANES) / LANES
     cos, sin = np.cos(lane_angle), np.sin(lane_angle)
     lanes_fwd = high_low(np.block([[cos, -sin], [sin, cos]]))
     lanes_inv = high_low(np.block([[cos, sin], [-sin, cos]]))
-    turn = np.pi * (2 * k1[:, None] + 1) * lane[None, :] / 131072.0
+    both = np.concatenate([k1, k1 + 512])
+    turn = np.pi * (2 * both[:, None] + 1) * lane[None, :] / 131072.0
     turns = np.stack([np.cos(turn), np.sin(turn)]).astype(np.float32)
     return rows_fwd, rows_inv, np.stack([lanes_fwd, lanes_inv]), turns
 
@@ -57,10 +57,10 @@
 
 
 def kernel(
-    signal_hbm, cotan_hbm, filter_hbm, rows_fwd_hbm, rows_inv_hbm, lanes_hbm, turns_hbm,
-    conv, corr, part_line,
-    signal_in, cotan_in, filter_in, rows_fwd, rows_inv, lanes_tab, turns,
-    stage, sent, got, mate, packed, spectrum, result,
+    signal_hbm, cotan_hbm, filter_hbm, skip_hbm, rows_fwd_hbm, rows_inv_hbm, lanes_hbm, turns_hbm,
+    conv, corr, part_line, cotan_in, skip_in,
+    signal_in, filter_in, rows_fwd, rows_inv, lanes_tab, turns,
+    stage, sent, got, mate, packed, mixed, spectrum, result,
     part, part_mate, part_plane, part_plane_sum,
     load_sem, table_sem, send_sem, recv_sem, mate_sems, out_send, conv_recv, corr_recv, part_send, part_recv, own_sem, cross_sem,
 ):
@@ -107,7 +107,7 @@
         ((signal_hbm, signal_in), (cotan_hbm, cotan_in), (filter_hbm, filter_in)), load_sem
     )
     table_loads = load_all(
-        ((rows_fwd_hbm, rows_fwd), (rows_inv_hbm, rows_inv), (lanes_hbm, lanes_tab), (turns_hbm, turns)),
+        ((rows_fwd_hbm, rows_fwd), (lanes_hbm, lanes_tab), (turns_hbm, turns), (rows_inv_hbm, rows_inv), (skip_hbm, skip_in)),
         table_sem,
     )
 
@@ -130,7 +130,7 @@
 
     def send(to):
         pltpu.make_async_remote_copy(
-            src_ref=sent.at[to], dst_ref=got.at[chip], send_sem=send_sem, recv_sem=recv_sem,
+            src_ref=sent.at[to], dst_ref=got.at[chip], send_sem=send_sem, recv_sem=recv_sem.at[z],
             device_id=(2 * to + core, chan), device_id_type=MESH,
         ).start()
 
@@ -159,16 +159,107 @@
 
     lax.fori_loop(1, 8, send_plane, 0)
 
-    all_but_one = got.at[pl.ds(0, CHIPS - 1)]
-    pltpu.make_async_copy(all_but_one, all_but_one, recv_sem).wait()
-
-    swap = pltpu.make_async_remote_copy(
-        src_ref=got.at[:, pl.ds(core, 2)], dst_ref=mate, send_sem=mate_sems.at[0], recv_sem=mate_sems.at[1],
-        device_id=mate_id, device_id_type=MESH,
+    def swap_slab(slab, chips):
+        arrived = got.at[pl.ds(8 * slab, chips)]
+        pltpu.make_async_copy(arrived, arrived, recv_sem.at[slab]).wait()
+        pltpu.make_async_remote_copy(
+            src_ref=got.at[pl.ds(8 * slab, 8), pl.ds(core, 2)], dst_ref=mate.at[pl.ds(8 * slab, 8)],
+            send_sem=mate_sems.at[0], recv_sem=mate_sems.at[1], device_id=mate_id, device_id_type=MESH,
+        ).start()
+
+    swap_slab(z, 7)
+
+    def swap_next(k, carry):
+        swap_slab((z + 8 + (2 * (k % 2) - 1) * ((k + 1) // 2)) % 8, 8)
+        return carry
+
+    lax.fori_loop(1, 8, swap_next, 0)
+    for load in table_loads:
+        load.wait()
+    pltpu.make_async_copy(mate, mate, mate_sems.at[1]).wait()
+
+    for k, (ours, theirs) in enumerate(((2 - 2 * core, other_core), (1, core))):
+        ours, theirs = got[:, ours].astype(F32), mate[:, theirs].astype(F32)
+        first = jnp.where(core == 0, ours, theirs)
+        second = jnp.where(core == 0, theirs, ours)
+        mixed[k] = jnp.concatenate([first, second], axis=1).reshape(ROWS, LANES)
+        for parity, group in enumerate(GROUPS):
+            for i, r in enumerate(group):
+                packed[parity, pl.ds(i * CHIPS, CHIPS), k * LANES : (k + 1) * LANES] = mixed[
+                    k, pl.ds(r, CHIPS, stride=8), :
+                ].astype(BF16)
+
+    even, odd = (
+        dot(rows_fwd[0, parity], packed[parity]) + dot(rows_fwd[1, parity], packed[parity]) for parity in range(2)
     )
-    swap.start()
-
-    pltpu.make_async_copy(all_but_one, all_but_one, send_sem).wait()
+    waves = jnp.concatenate([even[:HALF] + odd[:HALF], even[:HALF] - odd[:HALF]], axis=0)
+    waves_imag = jnp.concatenate([even[HALF:] + odd[HALF:], even[HALF:] - odd[HALF:]], axis=0)
+    cos, sin = turns[0], turns[1]
+    left = []
+    for k in range(2):
+        real, imag = waves[:, k * LANES : (k + 1) * LANES], waves_imag[:, k * LANES : (k + 1) * LANES]
+        left.append(jnp.concatenate([real * cos + imag * sin, imag * cos - real * sin], axis=1))
+    freq = three_pass(jnp.concatenate(left, axis=0), lanes_tab[0, 0], lanes_tab[0, 1])
+    b_real, b_imag = freq[:ROWS, :LANES], freq[:ROWS, LANES:]
+    g_real, g_imag = freq[ROWS:, :LANES], freq[ROWS:, LANES:]
+    product = jnp.concatenate([b_real * g_real + b_imag * g_imag, b_real * g_imag - b_imag * g_real], axis=1)
+    inner = three_pass(product, lanes_tab[1, 0], lanes_tab[1, 1])
+    real, imag = inner[:, :LANES], inner[:, LANES:]
+    real, imag = real * cos - imag * sin, imag * cos + real * sin
+    for parity in range(2):
+        sign = 1.0 - 2.0 * parity
+        for k, value in enumerate((real, imag)):
+            high, low = split(value[:HALF] + sign * value[HALF:])
+            spectrum[parity, pl.ds(k * HALF, HALF), :LANES] = high
+            spectrum[parity, pl.ds(k * HALF, HALF), LANES:] = low
+        wide = dot(rows_inv[0, parity], spectrum[parity])
+        value = wide[:, :LANES] + wide[:, LANES:] + dot(rows_inv[1, parity], spectrum[parity, :, :LANES])
+        for i, r in enumerate(GROUPS[parity]):
+            mixed[0, pl.ds(r, CHIPS, stride=8), :] = value[i * CHIPS : (i + 1) * CHIPS] * (2.0 / 131072.0)
+    result[...] = mixed[0].reshape(CHIPS, CORES, QUADS, LANES).astype(BF16)
+
+    def send_conv(to, c):
+        pltpu.make_async_remote_copy(
+            src_ref=result.at[to, c], dst_ref=conv.at[chip], send_sem=out_send, recv_sem=conv_recv,
+            device_id=(2 * to + c, chan), device_id_type=MESH,
+        ).start()
+
+    side = (home + chan) % 2
+
+    def send_corr(to, c):
+        pltpu.make_async_remote_copy(
+            src_ref=result.at[to, c], dst_ref=corr.at[side, chip % 32], send_sem=out_send, recv_sem=corr_recv.at[side],
+            device_id=(2 * to + c, home), device_id_type=MESH,
+        ).start()
+
+    own_conv = pltpu.make_async_copy(result.at[chip, core], conv.at[chip], own_sem.at[0])
+    own_corr = pltpu.make_async_copy(result.at[chip, core], corr.at[0, chip % 32], own_sem.at[0])
+
+    def send_half(half, order, send_to):
+        for k, step in enumerate(order):
+            z_to = 4 * half + (z + step) % 4
+            for dy, dx in plane_order:
+                to = in_plane(z_to, dy, dx)
+                if step or (dy, dx) != (0, 0) or k == 0:
+                    send_to(to, 0)
+                    send_to(to, 1)
+                else:
+                    send_to(to, other_core)
+
+    far_half, near_half = 1 - z // 4, z // 4
+    far_order, near_order = (0, 1, 3, 2), (2, 1, 3, 0)
+    @pl.when(core == 0)
+    def _():
+        send_half(far_half, far_order, send_conv)
+
+    @pl.when(jnp.logical_and(core == 1, not_home))
+    def _():
+        pl.semaphore_wait(cross_sem, 2)
+
+    @pl.when(core == 1)
+    def _():
+        send_half(far_half, far_order, send_corr)
+
     seven = part_plane.at[pl.ds(0, 7)]
     pltpu.make_async_copy(seven, seven, part_send.at[1]).wait()
     pltpu.make_async_copy(seven, seven, part_recv.at[1]).wait()
@@ -185,99 +276,7 @@
     lax.fori_loop(1, 8, send_line, 0)
     own_line = pltpu.make_async_copy(part_plane_sum, part_line.at[z], own_sem.at[1])
     own_line.start()
-    for load in table_loads:
-        load.wait()
-    swap.wait()
-
-    for k, (ours, theirs) in enumerate(((2 - 2 * core, other_core), (1, core))):
-        ours, theirs = got[:, ours].astype(F32), mate[:, theirs].astype(F32)
-        first = jnp.where(core == 0, ours, theirs)
-        second = jnp.where(core == 0, theirs, ours)
-        both = jnp.concatenate([first, second], axis=1)
-        packed[:, k * LANES : (k + 1) * LANES] = both.reshape(ROWS, LANES).astype(BF16)
-
-    def block(b, carry):
-        span = pl.ds(b * KBLOCK, KBLOCK)
-        cos, sin = turns[0, span, :], turns[1, span, :]
-        right = packed[...]
-        waves = dot(rows_fwd[0, b], right) + dot(rows_fwd[1, b], right)
-        real, imag = waves[:KBLOCK], waves[KBLOCK:]
-        cos2 = jnp.concatenate([cos, cos], axis=1)
-        sin2 = jnp.concatenate([sin, sin], axis=1)
-        real, imag = real * cos2 + imag * sin2, imag * cos2 - real * sin2
-        left = jnp.concatenate(
-            [
-                jnp.concatenate([real[:, :LANES], imag[:, :LANES]], axis=1),
-                jnp.concatenate([real[:, LANES:], imag[:, LANES:]], axis=1),
-            ],
-            axis=0,
-        )
-        freq = three_pass(left, lanes_tab[0, 0], lanes_tab[0, 1])
-        b_real, b_imag = freq[:KBLOCK, :LANES], freq[:KBLOCK, LANES:]
-        g_real, g_imag = freq[KBLOCK:, :LANES], freq[KBLOCK:, LANES:]
-        product = jnp.concatenate(
-            [b_real * g_real + b_imag * g_imag, b_real * g_imag - b_imag * g_real], axis=1
-        )
-        inner = three_pass(product, lanes_tab[1, 0], lanes_tab[1, 1])
-        real, imag = inner[:, :LANES], inner[:, LANES:]
-        real, imag = real * cos - imag * sin, imag * cos + real * sin
-        for k, value in enumerate((real, imag)):
-            high, low = split(value)
-            spectrum[pl.ds(k * ROWS + b * KBLOCK, KBLOCK), :LANES] = high
-            spectrum[pl.ds(k * ROWS + b * KBLOCK, KBLOCK), LANES:] = low
-        return carry
-
-    for b in range(ROWS // KBLOCK):
-        block(b, 0)
-
-    def rows_of(half):
-        wide = dot(rows_inv[0, half], spectrum[...])
-        value = wide[:, :LANES] + wide[:, LANES:] + dot(rows_inv[1, half], spectrum[:, :LANES])
-        result[pl.ds(32 * half, 32)] = (value * (2.0 / 131072.0)).reshape(CHIPS // 2, CORES, QUADS, LANES).astype(BF16)
-
-    def send_conv(to, c):
-        pltpu.make_async_remote_copy(
-            src_ref=result.at[to, c], dst_ref=conv.at[chip], send_sem=out_send, recv_sem=conv_recv,
-            device_id=(2 * to + c, chan), device_id_type=MESH,
-        ).start()
-
-    side = (home + chan) % 2
-
-    def send_corr(to, c):
-        pltpu.make_async_remote_copy(
-            src_ref=result.at[to, c], dst_ref=corr.at[side, chip % 32], send_sem=out_send, recv_sem=corr_recv.at[side],
-            device_id=(2 * to + c, home), device_id_type=MESH,
-        ).start()
-
-    own_conv = pltpu.make_async_copy(result.at[chip, core], conv.at[chip], own_sem.at[0])
-    own_corr = pltpu.make_async_copy(result.at[chip, core], corr.at[0, chip % 32], own_sem.at[0])
-
-    def send_half(half, order, send_to):
-        for k, step in enumerate(order):
-            z_to = 4 * half + (z + step) % 4
-            for dy, dx in plane_order:
-                to = in_plane(z_to, dy, dx)
-                send_to(to, other_core)
-                if step or (dy, dx) != (0, 0) or k == 0:
-                    send_to(to, core)
-
-    far_half, near_half = 1 - z // 4, z // 4
-    far_order, near_order = (0, 1, 3, 2), (2, 1, 3, 0)
-    rows_of(far_half)
-
-    @pl.when(core == 0)
-    def _():
-        send_half(far_half, far_order, send_conv)
-
-    @pl.when(jnp.logical_and(core == 1, not_home))
-    def _():
-        pl.semaphore_wait(cross_sem, 2)
-
-    @pl.when(core == 1)
-    def _():
-        send_half(far_half, far_order, send_corr)
-
-    rows_of(near_half)
+
 
     @pl.when(core == 0)
     def _():
@@ -298,6 +297,9 @@
     def _():
         send_corr(chip, core)
 
+    pltpu.make_async_copy(mate, mate, mate_sems.at[0]).wait()
+    all_but_one = got.at[pl.ds(0, CHIPS - 1)]
+    pltpu.make_async_copy(all_but_one, all_but_one, send_sem).wait()
     own_line.wait()
     line = part_line.at[pl.ds(0, 7)]
     pltpu.make_async_copy(line, line, part_send.at[2]).wait()
@@ -344,17 +346,18 @@
     rows_fwd, rows_inv, lanes_tab, turns = tables()
     vmem, anywhere = pl.BlockSpec(memory_space=pltpu.VMEM), pl.BlockSpec(memory_space=pl.ANY)
     dma = pltpu.SemaphoreType.DMA
-    conv, corr, part_line = pl.pallas_call(
+    landed = pl.pallas_call(
         kernel,
         out_shape=(
             pltpu.VMEM((CHIPS, QUADS, LANES), BF16),
             pltpu.VMEM((2, CHIPS // 2, QUADS, LANES), BF16),
             pltpu.VMEM((8, 8, LANES), F32),
+            pltpu.VMEM((CHIPS, ROWS), BF16),
+            pltpu.VMEM((1, CHIPS), F32),
         ),
-        in_specs=[anywhere] * 7,
-        out_specs=(vmem,) * 3,
+        in_specs=[anywhere] * 8,
+        out_specs=(vmem,) * 5,
         scratch_shapes=[
-            pltpu.VMEM((CHIPS, ROWS), BF16),
             pltpu.VMEM((CHIPS, ROWS), BF16),
             pltpu.VMEM((CHIPS, ROWS), BF16),
             pltpu.VMEM(rows_fwd.shape, BF16),
@@ -365,17 +368,18 @@
             pltpu.VMEM((CHIPS, 3, QUADS, LANES), BF16),
             pltpu.VMEM((CHIPS, 3, QUADS, LANES), BF16),
             pltpu.VMEM((CHIPS, 2, QUADS, LANES), BF16),
-            pltpu.VMEM((ROWS, 2 * LANES), BF16),
-            pltpu.VMEM((2 * ROWS, 2 * LANES), BF16),
+            pltpu.VMEM((2, HALF, 2 * LANES), BF16),
+            pltpu.VMEM((2, ROWS, LANES), F32),
+            pltpu.VMEM((2, ROWS, 2 * LANES), BF16),
             pltpu.VMEM((CHIPS, CORES, QUADS, LANES), BF16),
             pltpu.VMEM((8, LANES), F32),
             pltpu.VMEM((8, LANES), F32),
             pltpu.VMEM((8, 8, LANES), F32),
             pltpu.VMEM((8, LANES), F32),
             dma((3,)),
-            dma((4,)),
+            dma((5,)),
             dma,
-            dma,
+            dma((8,)),
             dma((2,)),
             dma,
             dma,
@@ -387,7 +391,7 @@
         ],
         compiler_params=pltpu.CompilerParams(collective_id=0, has_side_effects=True),
         name="hyena_backward",
-    )(signal, cotangent, filters, *(jnp.asarray(t) for t in (rows_fwd, rows_inv, lanes_tab, turns)))
+    )(signal, cotangent, filters, skip.reshape(1, CHIPS), *(jnp.asarray(t) for t in (rows_fwd, rows_inv, lanes_tab, turns)))
     signal_grad, filter_grad, skip_grad = pl.pallas_call(
         finish,
         out_shape=(
@@ -400,7 +404,7 @@
         scratch_shapes=[pltpu.VMEM((2, CHIPS * QUADS, LANES), F32)],
         name="finish",
         compiler_params=pltpu.CompilerParams(vmem_limit_bytes=8 * 1024 * 1024),
-    )(*(pltpu.with_memory_space_constraint(v, pltpu.VMEM) for v in (conv, corr, part_line)), cotangent, skip.reshape(1, CHIPS))
+    )(*(pltpu.with_memory_space_constraint(v, pltpu.VMEM) for v in landed))
     return signal_grad, filter_grad, skip_grad.reshape(CHIPS)
 
 

time: 34.5 us -> 34.2 us (level)
  no operation moved by 1% of the time
where the time goes in v4:
time: 34.2 us; the launch traced here: 34.1 us
  Pallas kernels  33.4 us (98%)
  between operations  0.64 us (2%)
    pallas_call x1, Pallas kernels, local(): pl.pallas_call(kernel, out_shape=(pltpu.VMEM((CHIPS, QUADS, LANES), BF16)...  32.7 us
    pallas_call x1, Pallas kernels, local(): pl.pallas_call(finish, out_shape=(jax.ShapeDtypeStruct((CHIPS, ROWS), BF1...  0.73 us

profile of v4, /device:TPU:1, one launch (start us, length us, event | category | flops | bytes accessed | tf_op | source)
XLA Modules:
  0.0 34.1 jit_solution(14321613725209905294)
XLA Ops:
  0.6 32.7 %hyena_backward.1 = (bf16[64,4,128]{2,1,0:T(4,128)(2,1)S(1)}, bf16[2,32,4,128]{3,2,1,0:T(4,128)(2,1)S(1)}, f32[8,8,128]{2,1,0:T(8,128)S(1)}, bf16[64,512]{1,0:T(8,128)(2,1)S(1)}, f32[1,64]{1,0:T(1,128)S(1)}) custom-call(bf16[64,512]{1,0:T(8,128)(2,1)} %signal_hbm.1, bf16[64,512]{1,0:T(8,128)(2,1)} %cotan_hbm.1, bf16[64,512]{1,0:T(8,128)(2,1)} %filter_hbm.1, ...), custom_call_target="tpu_custom_call" | custom-call | tf_op jit(solution)/shard_map/hyena_backward/pallas_call | solution.py:349
  33.3 0.7 %finish.1 = (bf16[64,512]{1,0:T(8,128)(2,1)}, f32[32,512]{1,0:T(8,128)}, f32[1,64]{1,0:T(1,128)}) custom-call(bf16[64,4,128]{2,1,0:T(4,128)(2,1)S(1)} %get-tuple-element.11.conv, bf16[2,32,4,128]{3,2,1,0:T(4,128)(2,1)S(1)} %get-tuple-element.12.corr, f32[8,8,128]{2,1,0:T(8,128)S(1)} %get-tuple-element.13.part_line, ...), custom_call_target="tpu_custom_call" | custom-call | tf_op jit(solution)/shard_map/finish/pallas_call | solution.py:395

commit v5 on v4

--- a/solution.py
+++ b/solution.py
@@ -34,12 +34,11 @@
     lane = np.arange(LANES)
     lane_angle = 2.0 * np.pi * (lane[:, None] * lane[None, :] % LANES) / LANES
     cos, sin = np.cos(lane_angle), np.sin(lane_angle)
-    lanes_fwd = high_low(np.block([[cos, -sin], [sin, cos]]))
-    lanes_inv = high_low(np.block([[cos, sin], [-sin, cos]]))
+    lanes_fwd, lanes_inv = np.block([[cos, -sin], [sin, cos]]), np.block([[cos, sin], [-sin, cos]])
     both = np.concatenate([k1, k1 + 512])
     turn = np.pi * (2 * both[:, None] + 1) * lane[None, :] / 131072.0
     turns = np.stack([np.cos(turn), np.sin(turn)]).astype(np.float32)
-    return rows_fwd, rows_inv, np.stack([lanes_fwd, lanes_inv]), turns
+    return rows_fwd, rows_inv, np.stack([lanes_fwd, lanes_inv]).astype(ml_dtypes.bfloat16), turns
 
 
 def split(x):
@@ -51,9 +50,8 @@
     return jnp.dot(a, b, preferred_element_type=F32)
 
 
-def three_pass(x, high, low):
-    x_high, x_low = split(x)
-    return dot(x_high, high) + dot(x_low, high) + dot(x_high, low)
+def one_pass(x, table):
+    return dot(x.astype(BF16), table)
 
 
 def kernel(
@@ -199,11 +197,11 @@
     for k in range(2):
         real, imag = waves[:, k * LANES : (k + 1) * LANES], waves_imag[:, k * LANES : (k + 1) * LANES]
         left.append(jnp.concatenate([real * cos + imag * sin, imag * cos - real * sin], axis=1))
-    freq = three_pass(jnp.concatenate(left, axis=0), lanes_tab[0, 0], lanes_tab[0, 1])
+    freq = one_pass(jnp.concatenate(left, axis=0), lanes_tab[0])
     b_real, b_imag = freq[:ROWS, :LANES], freq[:ROWS, LANES:]
     g_real, g_imag = freq[ROWS:, :LANES], freq[ROWS:, LANES:]
     product = jnp.concatenate([b_real * g_real + b_imag * g_imag, b_real * g_imag - b_imag * g_real], axis=1)
-    inner = three_pass(product, lanes_tab[1, 0], lanes_tab[1, 1])
+    inner = one_pass(product, lanes_tab[1])
     real, imag = inner[:, :LANES], inner[:, LANES:]
     real, imag = real * cos - imag * sin, imag * cos + real * sin
     for parity in range(2):

time: 34.2 us -> 33.2 us (0.971)
  Pallas kernels: 33.4 us -> 32.4 us
    pallas_call x1, Pallas kernels: 32.7 us -> 31.7 us  [local(): pl.pallas_call(kernel, out_shape=(pltpu.VMEM((CHIPS, QUADS, LANES), BF16)...]
where the time goes in v5:
time: 33.2 us; the launch traced here: 33.1 us
  Pallas kernels  32.4 us (98%)
  between operations  0.64 us (2%)
    pallas_call x1, Pallas kernels, local(): pl.pallas_call(kernel, out_shape=(pltpu.VMEM((CHIPS, QUADS, LANES), BF16)...  31.7 us
    pallas_call x1, Pallas kernels, local(): pl.pallas_call(finish, out_shape=(jax.ShapeDtypeStruct((CHIPS, ROWS), BF1...  0.73 us

profile of v5, /device:TPU:1, one launch (start us, length us, event | category | flops | bytes accessed | tf_op | source)
XLA Modules:
  0.0 33.1 jit_solution(14861525667140420019)
XLA Ops:
  0.6 31.7 %hyena_backward.1 = (bf16[64,4,128]{2,1,0:T(4,128)(2,1)S(1)}, bf16[2,32,4,128]{3,2,1,0:T(4,128)(2,1)S(1)}, f32[8,8,128]{2,1,0:T(8,128)S(1)}, bf16[64,512]{1,0:T(8,128)(2,1)S(1)}, f32[1,64]{1,0:T(1,128)S(1)}) custom-call(bf16[64,512]{1,0:T(8,128)(2,1)} %signal_hbm.1, bf16[64,512]{1,0:T(8,128)(2,1)} %cotan_hbm.1, bf16[64,512]{1,0:T(8,128)(2,1)} %filter_hbm.1, ...), custom_call_target="tpu_custom_call" | custom-call | tf_op jit(solution)/shard_map/hyena_backward/pallas_call | solution.py:347
  32.4 0.7 %finish.1 = (bf16[64,512]{1,0:T(8,128)(2,1)}, f32[32,512]{1,0:T(8,128)}, f32[1,64]{1,0:T(1,128)}) custom-call(bf16[64,4,128]{2,1,0:T(4,128)(2,1)S(1)} %get-tuple-element.11.conv, bf16[2,32,4,128]{3,2,1,0:T(4,128)(2,1)S(1)} %get-tuple-element.12.corr, f32[8,8,128]{2,1,0:T(8,128)S(1)} %get-tuple-element.13.part_line, ...), custom_call_target="tpu_custom_call" | custom-call | tf_op jit(solution)/shard_map/finish/pallas_call | solution.py:393

commit v6 on v5

--- a/solution.py
+++ b/solution.py
@@ -233,22 +233,21 @@
     own_conv = pltpu.make_async_copy(result.at[chip, core], conv.at[chip], own_sem.at[0])
     own_corr = pltpu.make_async_copy(result.at[chip, core], corr.at[0, chip % 32], own_sem.at[0])
 
-    def send_half(half, order, send_to):
-        for k, step in enumerate(order):
-            z_to = 4 * half + (z + step) % 4
-            for dy, dx in plane_order:
-                to = in_plane(z_to, dy, dx)
-                if step or (dy, dx) != (0, 0) or k == 0:
-                    send_to(to, 0)
-                    send_to(to, 1)
-                else:
-                    send_to(to, other_core)
-
-    far_half, near_half = 1 - z // 4, z // 4
-    far_order, near_order = (0, 1, 3, 2), (2, 1, 3, 0)
+    slab_order = (4, 3, 5, 2, 6, 1, 7, 0)
+
+    def send_all(send_to):
+        for c in range(CORES):
+            for dz in slab_order:
+                for dy, dx in plane_order:
+                    if dz or (dy, dx) != (0, 0):
+                        send_to(in_plane((z + dz) % 8, dy, dx), c)
+        send_to(chip, other_core)
+
     @pl.when(core == 0)
     def _():
-        send_half(far_half, far_order, send_conv)
+        send_all(send_conv)
+        own_conv.start()
+        own_conv.wait()
 
     @pl.when(jnp.logical_and(core == 1, not_home))
     def _():
@@ -256,7 +255,7 @@
 
     @pl.when(core == 1)
     def _():
-        send_half(far_half, far_order, send_corr)
+        send_all(send_corr)
 
     seven = part_plane.at[pl.ds(0, 7)]
     pltpu.make_async_copy(seven, seven, part_send.at[1]).wait()
@@ -274,17 +273,6 @@
     lax.fori_loop(1, 8, send_line, 0)
     own_line = pltpu.make_async_copy(part_plane_sum, part_line.at[z], own_sem.at[1])
     own_line.start()
-
-
-    @pl.when(core == 0)
-    def _():
-        send_half(near_half, near_order, send_conv)
-        own_conv.start()
-        own_conv.wait()
-
-    @pl.when(core == 1)
-    def _():
-        send_half(near_half, near_order, send_corr)
 
     @pl.when(jnp.logical_and(core == 1, is_home))
     def _():

time: 33.2 us -> 32.8 us (0.988)
  Pallas kernels: 32.4 us -> 32 us
    pallas_call x1, Pallas kernels: 31.7 us -> 31.3 us  [local(): pl.pallas_call(kernel, out_shape=(pltpu.VMEM((CHIPS, QUADS, LANES), BF16)...]
where the time goes in v6:
time: 32.8 us; the launch traced here: 32.7 us
  Pallas kernels  32 us (98%)
  between operations  0.64 us (2%)
    pallas_call x1, Pallas kernels, local(): pl.pallas_call(kernel, out_shape=(pltpu.VMEM((CHIPS, QUADS, LANES), BF16)...  31.3 us
    pallas_call x1, Pallas kernels, local(): pl.pallas_call(finish, out_shape=(jax.ShapeDtypeStruct((CHIPS, ROWS), BF1...  0.73 us

profile of v6, /device:TPU:1, one launch (start us, length us, event | category | flops | bytes accessed | tf_op | source)
XLA Modules:
  0.0 32.7 jit_solution(6726620188606131231)
XLA Ops:
  0.6 31.3 %hyena_backward.1 = (bf16[64,4,128]{2,1,0:T(4,128)(2,1)S(1)}, bf16[2,32,4,128]{3,2,1,0:T(4,128)(2,1)S(1)}, f32[8,8,128]{2,1,0:T(8,128)S(1)}, bf16[64,512]{1,0:T(8,128)(2,1)S(1)}, f32[1,64]{1,0:T(1,128)S(1)}) custom-call(bf16[64,512]{1,0:T(8,128)(2,1)} %signal_hbm.1, bf16[64,512]{1,0:T(8,128)(2,1)} %cotan_hbm.1, bf16[64,512]{1,0:T(8,128)(2,1)} %filter_hbm.1, ...), custom_call_target="tpu_custom_call" | custom-call | tf_op jit(solution)/shard_map/hyena_backward/pallas_call | solution.py:335
  32.0 0.7 %finish.1 = (bf16[64,512]{1,0:T(8,128)(2,1)}, f32[32,512]{1,0:T(8,128)}, f32[1,64]{1,0:T(1,128)}) custom-call(bf16[64,4,128]{2,1,0:T(4,128)(2,1)S(1)} %get-tuple-element.11.conv, bf16[2,32,4,128]{3,2,1,0:T(4,128)(2,1)S(1)} %get-tuple-element.12.corr, f32[8,8,128]{2,1,0:T(8,128)S(1)} %get-tuple-element.13.part_line, ...), custom_call_target="tpu_custom_call" | custom-call | tf_op jit(solution)/shard_map/finish/pallas_call | solution.py:381

commit v7 on v6

--- a/solution.py
+++ b/solution.py
@@ -73,16 +73,12 @@
     def in_plane(z_to, dy, dx):
         return (z_to * 4 + (y + dy) % 4) * 2 + (x + dx) % 2
 
+    steps = [(dz, dy, dx) for dz in range(8) for dy in range(4) for dx in range(2)]
+    steps.sort(key=lambda step: -(min(step[0], 8 - step[0]) + min(step[1], 4 - step[1]) + 2 * step[2]))
+
     def each_chip(visit):
-        def plane(k, carry):
-            z_to = (z + 4 + (1 - 2 * (k % 2)) * ((k + 1) // 2)) % 8
-            for dy, dx in plane_order:
-                visit(in_plane(z_to, dy, dx))
-            return carry
-
-        lax.fori_loop(0, 7, plane, 0)
-        for dy, dx in plane_order[:-1]:
-            visit(in_plane(z, dy, dx))
+        for dz, dy, dx in steps[:-1]:
+            visit(in_plane((z + dz) % 8, dy, dx))
 
     mate_id = (2 * chip + other_core, chan)
     barrier = pltpu.get_barrier_semaphore()
@@ -233,14 +229,11 @@
     own_conv = pltpu.make_async_copy(result.at[chip, core], conv.at[chip], own_sem.at[0])
     own_corr = pltpu.make_async_copy(result.at[chip, core], corr.at[0, chip % 32], own_sem.at[0])
 
-    slab_order = (4, 3, 5, 2, 6, 1, 7, 0)
 
     def send_all(send_to):
         for c in range(CORES):
-            for dz in slab_order:
-                for dy, dx in plane_order:
-                    if dz or (dy, dx) != (0, 0):
-                        send_to(in_plane((z + dz) % 8, dy, dx), c)
+            for dz, dy, dx in steps[:-1]:
+                send_to(in_plane((z + dz) % 8, dy, dx), c)
         send_to(chip, other_core)
 
     @pl.when(core == 0)

time: 32.8 us -> 32.2 us (0.982)
  Pallas kernels: 32 us -> 31.4 us
    pallas_call x1, Pallas kernels: 31.3 us -> 30.7 us  [local(): pl.pallas_call(kernel, out_shape=(pltpu.VMEM((CHIPS, QUADS, LANES), BF16)...]
where the time goes in v7:
time: 32.2 us; the launch traced here: 32.1 us
  Pallas kernels  31.4 us (98%)
  between operations  0.64 us (2%)
    pallas_call x1, Pallas kernels, local(): pl.pallas_call(kernel, out_shape=(pltpu.VMEM((CHIPS, QUADS, LANES), BF16)...  30.7 us
    pallas_call x1, Pallas kernels, local(): pl.pallas_call(finish, out_shape=(jax.ShapeDtypeStruct((CHIPS, ROWS), BF1...  0.73 us

profile of v7, /device:TPU:1, one launch (start us, length us, event | category | flops | bytes accessed | tf_op | source)
XLA Modules:
  0.0 32.1 jit_solution(18156519218448747367)
XLA Ops:
  0.6 30.7 %hyena_backward.1 = (bf16[64,4,128]{2,1,0:T(4,128)(2,1)S(1)}, bf16[2,32,4,128]{3,2,1,0:T(4,128)(2,1)S(1)}, f32[8,8,128]{2,1,0:T(8,128)S(1)}, bf16[64,512]{1,0:T(8,128)(2,1)S(1)}, f32[1,64]{1,0:T(1,128)S(1)}) custom-call(bf16[64,512]{1,0:T(8,128)(2,1)} %signal_hbm.1, bf16[64,512]{1,0:T(8,128)(2,1)} %cotan_hbm.1, bf16[64,512]{1,0:T(8,128)(2,1)} %filter_hbm.1, ...), custom_call_target="tpu_custom_call" | custom-call | tf_op jit(solution)/shard_map/hyena_backward/pallas_call | solution.py:328
  31.3 0.7 %finish.1 = (bf16[64,512]{1,0:T(8,128)(2,1)}, f32[32,512]{1,0:T(8,128)}, f32[1,64]{1,0:T(1,128)}) custom-call(bf16[64,4,128]{2,1,0:T(4,128)(2,1)S(1)} %get-tuple-element.11.conv, bf16[2,32,4,128]{3,2,1,0:T(4,128)(2,1)S(1)} %get-tuple-element.12.corr, f32[8,8,128]{2,1,0:T(8,128)S(1)} %get-tuple-element.13.part_line, ...), custom_call_target="tpu_custom_call" | custom-call | tf_op jit(solution)/shard_map/finish/pallas_call | solution.py:374

commit v8 on v7

--- a/solution.py
+++ b/solution.py
@@ -74,7 +74,11 @@
         return (z_to * 4 + (y + dy) % 4) * 2 + (x + dx) % 2
 
     steps = [(dz, dy, dx) for dz in range(8) for dy in range(4) for dx in range(2)]
-    steps.sort(key=lambda step: -(min(step[0], 8 - step[0]) + min(step[1], 4 - step[1]) + 2 * step[2]))
+
+    def hops(step):
+        return min(step[0], 8 - step[0]) + min(step[1], 4 - step[1]) + 2 * step[2]
+
+    steps.sort(key=lambda step: -hops(step))
 
     def each_chip(visit):
         for dz, dy, dx in steps[:-1]:
@@ -231,9 +235,9 @@
 
 
     def send_all(send_to):
-        for c in range(CORES):
-            for dz, dy, dx in steps[:-1]:
-                send_to(in_plane((z + dz) % 8, dy, dx), c)
+        targets = [(step, c) for step in steps[:-1] for c in range(CORES)]
+        for (dz, dy, dx), c in sorted(targets, key=lambda target: target[1] - hops(target[0])):
+            send_to(in_plane((z + dz) % 8, dy, dx), c)
         send_to(chip, other_core)
 
     @pl.when(core == 0)

time: 32.2 us -> 31.6 us (0.981)
  Pallas kernels: 31.4 us -> 30.8 us
    pallas_call x1, Pallas kernels: 30.7 us -> 30.1 us  [local(): pl.pallas_call(kernel, out_shape=(pltpu.VMEM((CHIPS, QUADS, LANES), BF16)...]
where the time goes in v8:
time: 31.6 us; the launch traced here: 31.5 us
  Pallas kernels  30.8 us (97%)
  between operations  0.64 us (2%)
    pallas_call x1, Pallas kernels, local(): pl.pallas_call(kernel, out_shape=(pltpu.VMEM((CHIPS, QUADS, LANES), BF16)...  30.1 us
    pallas_call x1, Pallas kernels, local(): pl.pallas_call(finish, out_shape=(jax.ShapeDtypeStruct((CHIPS, ROWS), BF1...  0.73 us

profile of v8, /device:TPU:1, one launch (start us, length us, event | category | flops | bytes accessed | tf_op | source)
XLA Modules:
  0.0 31.5 jit_solution(3436813170373922509)
XLA Ops:
  0.6 30.1 %hyena_backward.1 = (bf16[64,4,128]{2,1,0:T(4,128)(2,1)S(1)}, bf16[2,32,4,128]{3,2,1,0:T(4,128)(2,1)S(1)}, f32[8,8,128]{2,1,0:T(8,128)S(1)}, bf16[64,512]{1,0:T(8,128)(2,1)S(1)}, f32[1,64]{1,0:T(1,128)S(1)}) custom-call(bf16[64,512]{1,0:T(8,128)(2,1)} %signal_hbm.1, bf16[64,512]{1,0:T(8,128)(2,1)} %cotan_hbm.1, bf16[64,512]{1,0:T(8,128)(2,1)} %filter_hbm.1, ...), custom_call_target="tpu_custom_call" | custom-call | tf_op jit(solution)/shard_map/hyena_backward/pallas_call | solution.py:332
  30.7 0.7 %finish.1 = (bf16[64,512]{1,0:T(8,128)(2,1)}, f32[32,512]{1,0:T(8,128)}, f32[1,64]{1,0:T(1,128)}) custom-call(bf16[64,4,128]{2,1,0:T(4,128)(2,1)S(1)} %get-tuple-element.11.conv, bf16[2,32,4,128]{3,2,1,0:T(4,128)(2,1)S(1)} %get-tuple-element.12.corr, f32[8,8,128]{2,1,0:T(8,128)S(1)} %get-tuple-element.13.part_line, ...), custom_call_target="tpu_custom_call" | custom-call | tf_op jit(solution)/shard_map/finish/pallas_call | solution.py:378
